TPU v7x, 128 devices: a whole 4x4x4 slice. The times are simulated.
128 devices in a mesh: wide: 16 (over x, y_lo, core), narrow: 8 (over z, y_hi).
Axes of the slice: x: 4, y: 4 (y_hi: 2, y_lo: 2; y = y_hi * 2 + y_lo), z: 4, core: 2. Of those that a mesh axis runs over, the one named last changes fastest.
Arguments:
- positions: float32 [2, 1048576], P(None, ('wide', 'narrow')), may hold values from -1 to 1
- angles: float32 [1048576], P(('wide', 'narrow')), may hold values from -3.140625 to 3.140625
- weights: float32 [1048576], P(('wide', 'narrow')), may hold values from -6 to 6
- owner_dev: int32 [1048576, 1], P(('wide', 'narrow')), may hold values from 0 to 127; in each aligned block of 8192 rows (0 to 8191, 8192 to 16383, ...) at most 256 rows name the same one
- leaf_slot: int32 [1048576], P(('wide', 'narrow')), may hold values from 0 to 255
- phase_table: float32 [5, 32768, 256], P(None, ('wide', 'narrow')), may hold values from -3.140625 to 3.140625
Outputs:
- radon_field: float32 [32768, 512], P(('wide', 'narrow'))
Inputs may be any that keep to these rules, and one draw needn't show every extreme that they name: `owner_dev`: among the rows of one device no owner is named more than 256 times, and in every draw some owner is named exactly 256 times by the rows of some device.
All inputs are finite; a program needn't handle non-finite values.
Results may differ from a plain program's by a relative error of at most 0.0003.
Values sent between devices are 32-bit elements; how exact they have to be, the bound alone decides.
A program may use at most 128 MiB of HBM per device.

v0:
```python
import math

import jax
import jax.numpy as jnp
from jax import lax
from jax.sharding import PartitionSpec as P

Q = 16


LEAF_GAIN = 5.0
SQRT_HALF = 0.7071067811865476
HIGH = lax.Precision.HIGHEST


def partner_2(value, axis, apart):
    return lax.ppermute(value, axis, [(i, i ^ 1 << apart) for i in range(lax.axis_size(axis))])


def cheb_nodes(grid_order):
    counter = jnp.arange(grid_order, dtype=jnp.float32)
    return jnp.cos((2.0 * counter + 1.0) * math.pi / (2.0 * grid_order))


def lagrange(points, grid_order):
    node_list = cheb_nodes(grid_order)
    offsets = points[..., None] - node_list
    unit_col = jnp.ones_like(offsets[..., :1])
    before = jnp.cumprod(jnp.concatenate([unit_col, offsets[..., :-1]], -1), -1)
    after_prod = jnp.flip(
        jnp.cumprod(jnp.concatenate([unit_col, jnp.flip(offsets[..., 1:], -1)], -1), -1), -1
    )
    node_gaps = node_list[:, None] - node_list[None, :] + jnp.eye(grid_order, dtype=jnp.float32)
    node_prod = jnp.prod(node_gaps, 1)
    return before * after_prod / node_prod


def interp_kron(grid_order, side_value):
    node_list = cheb_nodes(grid_order)
    interp = lagrange((node_list + (2.0 * side_value - 1.0)) * 0.5, grid_order)
    return (interp[:, None, :, None] * interp[None, :, None, :]).reshape(
        grid_order * grid_order, grid_order * grid_order
    )


def apply_kron(coeffs, kron_matrix):
    flat_rows = coeffs.reshape(-1, kron_matrix.shape[0])
    result = lax.dot_general(
        flat_rows,
        kron_matrix,
        (((1,), (1,)), ((), ())),
        precision=HIGH,
        preferred_element_type=jnp.float32,
    )
    return result.reshape(coeffs.shape)


def rotate(coeffs, angle_rows):
    half_width = angle_rows.shape[-1]
    real_part = coeffs[..., :half_width]
    imag_part = coeffs[..., half_width:]
    cosine = jnp.cos(angle_rows)
    sine_val = jnp.sin(angle_rows)
    return jnp.concatenate(
        [cosine * real_part - sine_val * imag_part, sine_val * real_part + cosine * imag_part], -1
    )


def leaf_terms(first_pos, second_pos, phase_angle, weight, grid_order):
    first_basis = lagrange(first_pos, grid_order)
    second_basis = lagrange(second_pos, grid_order)
    outer_prod = (first_basis[:, :, None] * second_basis[:, None, :]).reshape(
        -1, grid_order * grid_order
    ) * (LEAF_GAIN * weight)[:, None]
    return jnp.concatenate(
        [outer_prod * jnp.cos(phase_angle)[:, None], outer_prod * jnp.sin(phase_angle)[:, None]], 1
    )


def combine(own_coeffs, pair_coeffs, side_bit, kron_zero, kron_one):
    kron_own = jnp.where(side_bit == 1, kron_one, kron_zero)
    kron_pair = jnp.where(side_bit == 1, kron_zero, kron_one)
    return SQRT_HALF * (apply_kron(own_coeffs, kron_own) + apply_kron(pair_coeffs, kron_pair))


def shards(positions, angles, weights, owner_dev, leaf_slot, phase_table):
    grid_order = Q
    points_sq = grid_order * grid_order
    wide_count = lax.axis_size("wide")
    narrow_count = lax.axis_size("narrow")
    devices = wide_count * narrow_count
    source_count = angles.shape[0]
    capacity = 4 * source_count // devices
    slot_count = devices * capacity
    box_count = phase_table.shape[1]
    target_dev = owner_dev[:, 0]
    dev_tags = jnp.arange(devices, dtype=jnp.int32)
    dev_counts = jnp.sum((target_dev[:, None] == dev_tags[None, :]).astype(jnp.int32), 0)
    dev_starts = jnp.cumsum(dev_counts) - dev_counts
    source_order = jnp.argsort(target_dev, stable=True)
    rank_grid = jnp.arange(capacity, dtype=jnp.int32)[None, :]
    slot_valid = (rank_grid < dev_counts[:, None]).reshape(slot_count)
    slot_pick = jnp.minimum(dev_starts[:, None] + rank_grid, source_count - 1).reshape(slot_count)
    slot_source = jnp.take(source_order, slot_pick, axis=0)
    records = jnp.stack([positions[0], positions[1], angles, weights])
    float_send = jnp.where(slot_valid[None, :], jnp.take(records, slot_source, axis=1), 0.0)
    index_send = jnp.where(slot_valid, jnp.take(leaf_slot, slot_source, axis=0), 0)[None, :]
    float_recv, index_recv = (
        lax.all_to_all(float_send, ("wide", "narrow"), split_axis=1, concat_axis=1, tiled=True),
        lax.all_to_all(index_send, ("wide", "narrow"), split_axis=1, concat_axis=1, tiled=True),
    )
    block_rows = math.gcd(slot_count, 2048)
    box_tags = jnp.arange(box_count, dtype=jnp.int32)

    def add_block(block_no, running):
        start = block_no * block_rows
        block_recs = lax.dynamic_slice_in_dim(float_recv, start, block_rows, 1)
        block_ids = lax.dynamic_slice_in_dim(index_recv[0], start, block_rows, 0)
        term_rows = leaf_terms(
            block_recs[0], block_recs[1], block_recs[2], block_recs[3], grid_order
        )
        one_hot = (block_ids[:, None] == box_tags[None, :]).astype(jnp.float32)
        return running + lax.dot_general(
            one_hot,
            term_rows,
            (((0,), (0,)), ((), ())),
            precision=HIGH,
            preferred_element_type=jnp.float32,
        )

    coeffs = lax.fori_loop(
        0, slot_count // block_rows, add_block, jnp.zeros((box_count, 2 * points_sq), jnp.float32)
    )
    kron_zero = interp_kron(grid_order, 0.0)
    kron_one = interp_kron(grid_order, 1.0)
    narrow_index = lax.axis_index("narrow")
    wide_index = lax.axis_index("wide")
    for bit_index in (0, 1):
        side_bit = jnp.bitwise_and(jnp.right_shift(narrow_index, bit_index), 1)
        rotated = rotate(coeffs, phase_table[bit_index])
        partner = partner_2(rotated, "narrow", bit_index)
        coeffs = combine(rotated, partner, side_bit, kron_zero, kron_one)
    top_bit = wide_count.bit_length() - 2
    for level_no, bit_index in ((2, 0), (3, 1), (4, top_bit)):
        side_bit = jnp.bitwise_and(jnp.right_shift(wide_index, bit_index), 1)
        rotated = rotate(coeffs, phase_table[level_no])
        partner = partner_2(rotated, "wide", bit_index)
        coeffs = combine(rotated, partner, side_bit, kron_zero, kron_one)
    return coeffs


def solution(mesh):
    placed = (
        P(None, ("wide", "narrow")),
        P(("wide", "narrow")),
        P(("wide", "narrow")),
        P(("wide", "narrow"), None),
        P(("wide", "narrow")),
        P(None, ("wide", "narrow"), None),
    )
    return jax.shard_map(
        shards, mesh=mesh, in_specs=placed, out_specs=P(("wide", "narrow"), None), check_vma=False
    )
```

profile of v0, /device:TPU:1, one launch (start us, length us, event | category | flops | bytes accessed | tf_op | source)
XLA Modules:
  0.0 733.4 jit_solution(16972279108802460094)
XLA Ops:
  0.0 4.3 convert_reduce_fusion
  4.4 7.5 %sort.17 = (s32[8192]{0:T(1024)}, s32[8192]{0:T(1024)S(1)}) sort(s32[8192]{0:T(1024)} %bitcast.162, s32[8192]{0:T(1024)S(1)} %iota.112), dimensions={0}, to_apply=%region_1.0 | sort | flops 106496 | bytes 131072 | tf_op jit(solution)/shard_map/jit(argsort)/sort | solution.py:100
  12.6 180.5 %gather_fusion.1 = s32[32768]{0:T(1024)S(1)} fusion(s32[8192]{0:T(1024)S(1)} %get-tuple-element.155, s32[32768]{0:T(1024)S(1)} %fusion.30), kind=kCustom, calls=%fused_computation.clone | custom fusion | bytes 393216 | tf_op jit(solution)/shard_map/jit(_take)/gather | solution.py:104
  193.2 180.5 %gather_fusion.2 = s32[32768]{0:T(1024)S(1)} fusion(s32[8192]{0:T(1024)S(1)} %copy-done, s32[32768]{0:T(1024)S(1)} %broadcast_clamp_fusion), kind=kCustom, calls=%fused_computation.1.clone | custom fusion | bytes 393216 | tf_op jit(solution)/shard_map/jit(_take)/gather | solution.py:107
  374.5 11.5 %all-to-all-start = ((s32[1,128,256]{2,0,1:T(1,128)}), s32[1,128,256]{2,0,1:T(1,128)S(1)}, u32[]{:S(2)}, u32[]{:S(2)}) async-start(s32[1,128,256]{2,0,1:T(1,128)} %bitcast.7), calls=%async_computation | async-start | bytes 262144 | tf_op jit(solution)/shard_map/all_to_all | solution.py:110
  386.2 2.6 copy.21
  388.8 110.4 %gather_fusion = f32[32768,4]{1,0:T(8,128)} fusion(f32[4,8192]{0,1:T(8,128)} %copy.21, s32[32768]{0:T(1024)S(1)} %broadcast_clamp_fusion), kind=kCustom, calls=%fused_computation.2 | custom fusion | bytes 1179648 | tf_op jit(solution)/shard_map/jit(_take)/gather | solution.py:106
  499.2 9.5 %copy.22 = f32[4,128,256]{2,0,1:T(4,128)S(1)} copy(f32[4,128,256]{0,2,1:T(8,128)} %bitcast.149) | data formatting | bytes 1048576 | tf_op jit(solution)/shard_map/jit(_take)/gather | solution.py:106
  509.9 10.3 %all-to-all-start.1 = ((f32[4,128,256]{2,0,1:T(4,128)}), f32[4,128,256]{2,0,1:T(4,128)S(1)}, u32[]{:S(2)}, u32[]{:S(2)}) async-start(f32[4,128,256]{2,0,1:T(4,128)} %select_select_fusion), calls=%async_computation.1 | async-start | bytes 1048576 | tf_op jit(solution)/shard_map/all_to_all | solution.py:109
  521.5 12.6 %all-to-all-done.1 = f32[4,128,256]{2,0,1:T(4,128)S(1)} async-done(((f32[4,128,256]{2,0,1:T(4,128)}), f32[4,128,256]{2,0,1:T(4,128)S(1)}, u32[]{:S(2)}, u32[]{:S(2)}) %all-to-all-start.1) | async-done | bytes 524320 | tf_op jit(solution)/shard_map/all_to_all | solution.py:109
  534.1 104.5 %while.17 = (s32[]{:T(128)}, f32[256,512]{1,0:T(8,128)S(1)}, s32[1,32768]{1,0:T(1,128)S(1)}, f32[4,32768]{1,0:T(4,128)S(1)}, s32[]{:T(128)}, /*index=5*/s32[]{:T...) while((s32[]{:T(128)}, f32[256,512]{1,0:T(8,128)S(1)}, ...), condition=%wide.region_9.11_spmd.clone, body=%wide.region_3.10_spmd.clone.sunk | while | flops 3227847936 | bytes 18096700 | solution.py:131
  537.6 3.0 fusion.69
  544.2 3.0 fusion.69
  550.7 3.0 fusion.69
  557.2 3.0 fusion.69
  563.8 3.0 fusion.69
  570.3 3.0 fusion.69
  576.8 3.0 fusion.69
  583.4 3.0 fusion.69
  589.9 3.0 fusion.69
  596.4 3.0 fusion.69
  603.0 3.0 fusion.69
  609.5 3.0 fusion.69
  616.0 3.0 fusion.69
  622.6 3.0 fusion.69
  629.1 3.0 fusion.69
  635.6 3.0 fusion.69
  638.7 1.9 fusion.28
  641.2 7.0 multiply_select_fusion
  648.2 2.4 select_n.187
  650.7 3.1 select_n.185
  654.6 1.7 fusion.35
  656.3 1.1 reshape.412
  657.5 1.4 fusion.19
  658.9 1.2 mul.560
  660.1 1.9 fusion.26
  662.7 2.4 select_n.192
  665.2 3.1 select_n.190
  669.1 1.7 fusion.36
  670.8 3.5 collective-permute-done.1
  674.3 1.1 reshape.414
  675.5 1.4 fusion.18
  676.9 1.2 mul.566
  678.1 1.9 fusion.24
  680.1 2.5 collective-permute-start.2
  682.6 2.4 select_n.197
  685.0 3.1 select_n.195
  689.0 1.7 fusion.37
  690.7 1.1 reshape.416
  691.9 1.4 fusion.17
  693.3 1.2 mul.572
  694.5 1.9 fusion.22
  696.5 1.2 collective-permute-start.3
  697.6 2.4 select_n.202
  700.1 3.1 select_n.200
  704.0 1.7 fusion.38
  705.7 4.7 collective-permute-done.3
  710.4 1.1 reshape.418
  711.5 1.4 fusion.16
  712.9 1.2 mul.578
  714.1 1.9 fusion.20
  716.7 2.4 select_n.207
  720.8 9.7 %collective-permute-done.4 = f32[256,512]{1,0:T(8,128)} collective-permute-done((f32[256,512]{1,0:T(8,128)S(1)}, f32[256,512]{1,0:T(8,128)}, u32[]{:S(2)}, u32[]{:S(2)}) %collective-permute-start.4) | collective-permute-done | bytes 524320 | tf_op jit(solution)/shard_map/ppermute | solution.py:17
  730.5 1.1 reshape.420
  (332 shorter events, 67.3 us)
Async XLA Ops:
  0.0 193.2 %copy-start = (s32[8192]{0:T(1024)S(1)}, s32[8192]{0:T(1024)}, u32[]{:S(2)}) copy-start(s32[8192]{0:T(1024)} %param.14) | copy-start | bytes 98308
  193.2 192.9 %copy-start.2 = (f32[2,8192]{1,0:T(2,128)S(1)}, f32[2,8192]{1,0:T(2,128)}, u32[]{:S(2)}) copy-start(f32[2,8192]{1,0:T(2,128)} %param.10) | copy-start | bytes 196612
  193.2 192.9 %copy-start.3 = (f32[8192]{0:T(1024)S(1)}, f32[8192]{0:T(1024)}, u32[]{:S(2)}) copy-start(f32[8192]{0:T(1024)} %param.12) | copy-start | bytes 98308
  193.2 192.9 %copy-start.4 = (f32[8192]{0:T(1024)S(1)}, f32[8192]{0:T(1024)}, u32[]{:S(2)}) copy-start(f32[8192]{0:T(1024)} %param.11) | copy-start | bytes 98308
  374.5 135.4 %all-to-all-start = ((s32[1,128,256]{2,0,1:T(1,128)}), s32[1,128,256]{2,0,1:T(1,128)S(1)}, u32[]{:S(2)}, u32[]{:S(2)}) async-start(s32[1,128,256]{2,0,1:T(1,128)} %bitcast.7), calls=%async_computation | async-start | bytes 262144 | tf_op jit(solution)/shard_map/all_to_all | solution.py:110
  509.9 24.3 %all-to-all-start.1 = ((f32[4,128,256]{2,0,1:T(4,128)}), f32[4,128,256]{2,0,1:T(4,128)S(1)}, u32[]{:S(2)}, u32[]{:S(2)}) async-start(f32[4,128,256]{2,0,1:T(4,128)} %select_select_fusion), calls=%async_computation.1 | async-start | bytes 1048576 | tf_op jit(solution)/shard_map/all_to_all | solution.py:109
  640.6 15.7 %collective-permute-start = (f32[256,512]{1,0:T(8,128)S(1)}, f32[256,512]{1,0:T(8,128)}, u32[]{:S(2)}, u32[]{:S(2)}) collective-permute-start(f32[256,512]{1,0:T(8,128)S(1)} %pad_maximum_fusion), channel_id=1, source_target_pairs={{0,1},{1,0},{2,3},{3,2},{4,5},{5,4},{6,7},{7,6},{8,9},{9,8},{10,11... | collective-permute-start | bytes 1572872 | tf_op jit(solution)/shard_map/ppermute | solution.py:17
  662.1 12.2 %collective-permute-start.1 = (f32[256,512]{1,0:T(8,128)S(1)}, f32[256,512]{1,0:T(8,128)}, u32[]{:S(2)}, u32[]{:S(2)}) collective-permute-start(f32[256,512]{1,0:T(8,128)S(1)} %pad_maximum_fusion.1), channel_id=1, source_target_pairs={{0,2},{1,3},{2,0},{3,1},{4,6},{5,7},{6,4},{7,5},{8,10},{9,11},{10,... | collective-permute-start | bytes 1572872 | tf_op jit(solution)/shard_map/ppermute | solution.py:17
  680.1 10.7 %collective-permute-start.2 = (f32[256,512]{1,0:T(8,128)S(1)}, f32[256,512]{1,0:T(8,128)}, u32[]{:S(2)}, u32[]{:S(2)}) collective-permute-start(f32[256,512]{1,0:T(8,128)S(1)} %pad_maximum_fusion.2), channel_id=1, source_target_pairs={{0,8},{8,0},{16,24},{24,16},{32,40},{40,32},{48,56},{56,48},{64,72... | collective-permute-start | bytes 1572872 | tf_op jit(solution)/shard_map/ppermute | solution.py:17
  696.5 13.9 %collective-permute-start.3 = (f32[256,512]{1,0:T(8,128)S(1)}, f32[256,512]{1,0:T(8,128)}, u32[]{:S(2)}, u32[]{:S(2)}) collective-permute-start(f32[256,512]{1,0:T(8,128)S(1)} %pad_maximum_fusion.3), channel_id=1, source_target_pairs={{0,16},{8,24},{16,0},{24,8},{32,48},{40,56},{48,32},{56,40},{64,80... | collective-permute-start | bytes 1572872 | tf_op jit(solution)/shard_map/ppermute | solution.py:17
  716.1 14.3 %collective-permute-start.4 = (f32[256,512]{1,0:T(8,128)S(1)}, f32[256,512]{1,0:T(8,128)}, u32[]{:S(2)}, u32[]{:S(2)}) collective-permute-start(f32[256,512]{1,0:T(8,128)S(1)} %pad_maximum_fusion.4), channel_id=1, source_target_pairs={{0,64},{8,72},{16,80},{24,88},{32,96},{40,104},{48,112},{56,120},{... | collective-permute-start | bytes 1572872 | tf_op jit(solution)/shard_map/ppermute | solution.py:17
  720.2 13.0 %copy-start.1 = (s32[8192]{0:T(1024)S(1)}, s32[8192]{0:T(1024)}, u32[]{:S(2)}) copy-start(s32[8192]{0:T(1024)} %param.14) | copy-start | bytes 98308
where the time goes:
time: 741 us; the launch traced here: 733 us
  local copies, waits for them, and re-layouts  547 us (74%)
  other arithmetic  63.9 us (9%)
  matrix products  62.1 us (8%)
  waiting for transfers between devices  30.5 us (4%)
  starting transfers between devices  27.3 us (4%)
    gather x1, local copies, waits for them, and re-layouts, shards(): slot_source = jnp.take(source_order, slot_pick, axis=0)  181 us
    gather x1, local copies, waits for them, and re-layouts, shards(): jnp.take(leaf_slot, slot_source, axis=0)  181 us
    gather x2, local copies, waits for them, and re-layouts, shards(): jnp.take(records, slot_source, axis=1)  120 us
    dot_general x16, matrix products, add_block(): lax.dot_general(one_hot, term_rows, (((0,), (0,)), ((), ())), precision=H...  48.3 us
    ppermute x5, waiting for transfers between devices, partner_2(): lax.ppermute(value, axis, [(i, i ^ 1 << apart) for i in range(lax.axis_si...  17.9 us
  transfers between devices with their start and end apart: 7, of which 4 were waited for; matrix products, arithmetic and copies ran while one was open for 23% of the time, Pallas kernels for 0%

commit v1 on v0

--- a/solution.py
+++ b/solution.py
@@ -1,8 +1,12 @@
+import functools
 import math
 
 import jax
 import jax.numpy as jnp
+import numpy as np
 from jax import lax
+from jax.experimental import pallas as pl
+from jax.experimental.pallas import tpu as pltpu
 from jax.sharding import PartitionSpec as P
 
 Q = 16
@@ -11,6 +15,22 @@
 LEAF_GAIN = 5.0
 SQRT_HALF = 0.7071067811865476
 HIGH = lax.Precision.HIGHEST
+MESH = pl.DeviceIdType.MESH
+DEVICES = 128
+RANKS = 128
+FIELDS = 5
+LEVELS = 5
+SOURCES = 8192
+LANES = 128
+POINTS = 256
+PARTS = 11
+STEP = 8
+GROUP = 8
+GROUPS = DEVICES // GROUP
+ROW_BITS = ((0, 6), (1, 5), (3, 4), (4, 3), (6, 2), (2, 1), (5, 0))
+STEP_BITS = ((6, 6), (5, 2), (4, 0), (3, 5), (2, 1), (1, 4), (0, 3))
+BF = jnp.bfloat16
+F32 = jnp.float32
 
 
 def partner_2(value, axis, apart):
@@ -83,7 +103,7 @@
     return SQRT_HALF * (apply_kron(own_coeffs, kron_own) + apply_kron(pair_coeffs, kron_pair))
 
 
-def shards(positions, angles, weights, owner_dev, leaf_slot, phase_table):
+def plain(positions, angles, weights, owner_dev, leaf_slot, phase_table):
     grid_order = Q
     points_sq = grid_order * grid_order
     wide_count = lax.axis_size("wide")
@@ -149,6 +169,396 @@
     return coeffs
 
 
+NODES = np.cos((2 * np.arange(Q) + 1) * np.pi / (2 * Q))
+GAPS = np.prod(NODES[:, None] - NODES[None, :] + np.eye(Q), 1)
+
+
+def kron_table():
+    blocks = []
+    for side in (0.0, 1.0):
+        points = (NODES + 2.0 * side - 1.0) * 0.5
+        offsets = points[:, None] - NODES
+        basis = np.stack(
+            [np.prod(np.delete(offsets, k, 1), 1) / GAPS[k] for k in range(Q)], 1
+        )
+        blocks.append(np.kron(basis, basis).T)
+    table = np.concatenate(blocks, 0) * SQRT_HALF
+    high = table.astype(np.float32).astype(BF)
+    low = (table - high.astype(np.float64)).astype(np.float32).astype(BF)
+    return high, low
+
+
+def series(function, degree):
+    fit = np.polynomial.chebyshev.Chebyshev.interpolate(
+        lambda t: function(np.sqrt(t)), degree, domain=[0.0, np.pi**2]
+    )
+    return [float(c) for c in fit.convert(kind=np.polynomial.Polynomial).coef]
+
+
+COS_SERIES = series(np.cos, 7)
+SIN_SERIES = series(lambda x: np.sinc(x / np.pi), 7)
+
+
+def cos_sin(angle):
+    square = angle * angle
+    cosine = jnp.full_like(angle, COS_SERIES[-1])
+    for c in COS_SERIES[-2::-1]:
+        cosine = cosine * square + c
+    sine = jnp.full_like(angle, SIN_SERIES[-1])
+    for c in SIN_SERIES[-2::-1]:
+        sine = sine * square + c
+    return cosine, sine * angle
+
+
+def basis_rows(points):
+    offsets = [points - float(t) for t in NODES]
+    before = [None, offsets[0]]
+    for k in range(1, Q - 1):
+        before.append(before[-1] * offsets[k])
+    after = [None, offsets[Q - 1]]
+    for k in range(Q - 2, 0, -1):
+        after.append(after[-1] * offsets[k])
+    after = after[::-1]
+    rows = []
+    for k in range(Q):
+        scale = float(1.0 / GAPS[k])
+        if k == 0:
+            rows.append(after[0] * scale)
+        elif k == Q - 1:
+            rows.append(before[k] * scale)
+        else:
+            rows.append(before[k] * after[k] * scale)
+    return rows
+
+
+def split(value, count):
+    parts = []
+    for _ in range(count - 1):
+        part = value.astype(BF).astype(F32)
+        parts.append(part)
+        value = value - part
+    return parts + [value]
+
+
+def move_bits(value, table):
+    out = None
+    for source, target in table:
+        bit = lax.shift_left(
+            lax.bitwise_and(lax.shift_right_logical(value, jnp.int32(source)), jnp.int32(1)),
+            jnp.int32(target),
+        )
+        out = bit if out is None else lax.bitwise_or(out, bit)
+    return out
+
+
+def dot_nt(left, right):
+    return lax.dot_general(left, right, (((1,), (1,)), ((), ())), preferred_element_type=F32)
+
+
+def dot_nn(left, right):
+    return jnp.dot(left, right, preferred_element_type=F32)
+
+
+def body(
+    pos, ang, wgt, own, slot, phase, high_k, low_k,
+    out, flag,
+    pair_s, box_s, wc_s, ws_s, left_s, right_s, packed_s,
+    send_rec, recv_rec, send_ph, recv_ph, send_out,
+    basis_v, basis_c, basis_s, terms_s, hot_s, leaf_s, state_s,
+    rec_send, rec_recv, ph_send, ph_recv, out_send, out_recv, own_sem,
+):
+    me = lax.axis_index("wide") * 8 + lax.axis_index("narrow")
+    my_row = move_bits(me, ROW_BITS)
+
+    def device(t):
+        return {"wide": lax.shift_right_logical(t, 3), "narrow": lax.bitwise_and(t, 7)}
+
+    def partner_at(step):
+        return lax.bitwise_xor(me, move_bits(step, STEP_BITS))
+
+    barrier = pltpu.get_barrier_semaphore()
+
+    def greet(step, carry):
+        pl.semaphore_signal(
+            barrier, inc=1, device_id=device(partner_at(step)), device_id_type=MESH
+        )
+        return carry
+
+    lax.fori_loop(1, DEVICES, greet, 0)
+
+    for level in range(LEVELS):
+        for k in range(2):
+            send_ph[level, pl.ds(k, 256, stride=2), :] = phase[level, :, k * LANES : (k + 1) * LANES]
+
+    slots = slot[...]
+    pair_s[...] = lax.shift_right_logical(slots, 1)
+    box_s[...] = (
+        move_bits(own[...], ROW_BITS) * 2 + lax.bitwise_and(slots, 1)
+    ).astype(F32)
+    cosine, sine = cos_sin(ang[...])
+    gain = wgt[...] * LEAF_GAIN
+    wc_s[...] = gain * cosine
+    ws_s[...] = gain * sine
+    packed_s[...] = jnp.zeros_like(packed_s)
+
+    row_128 = lax.broadcasted_iota(jnp.int32, (128, LANES), 0)
+    row_64 = lax.broadcasted_iota(jnp.int32, (64, LANES), 0)
+    row_256f = lax.broadcasted_iota(jnp.int32, (256, LANES), 0).astype(F32)
+    before = lax.broadcasted_iota(jnp.int32, (LANES, 256), 0)
+    column = lax.broadcasted_iota(jnp.int32, (LANES, 256), 1)
+    counter = jnp.where((before < column) | (column >= LANES), 1.0, 0.0).astype(BF)
+
+    def pack(block, counts):
+        for j in range(STEP):
+            c = block * STEP + j
+            lanes = slice(j * LANES, (j + 1) * LANES)
+            pair = pair_s[pl.ds(c, 1), :]
+            named = row_128 == pair
+            seen = dot_nn(jnp.where(named, 1.0, 0.0).astype(BF), counter)
+            rank = jnp.sum(
+                jnp.where(named, seen[:, :LANES] + counts, 0.0), axis=0, keepdims=True
+            )
+            counts = counts + seen[:, LANES:]
+            high_pair = lax.shift_right_logical(pair, 6).astype(F32) * RANKS
+            place = jnp.where(rank < RANKS, high_pair + rank, -1.0)
+            right_s[:, lanes] = jnp.where(row_256f == place, 1.0, 0.0).astype(BF)
+            low_pair = row_64 == lax.bitwise_and(pair, 63)
+            start = pl.multiple_of(c * LANES, LANES)
+            values = (
+                split(pos[0:1, pl.ds(start, LANES)], 3)
+                + split(pos[1:2, pl.ds(start, LANES)], 3)
+                + split(wc_s[pl.ds(c, 1), :], 2)
+                + split(ws_s[pl.ds(c, 1), :], 2)
+                + [box_s[pl.ds(c, 1), :]]
+            )
+            for p, value in enumerate(values):
+                left_s[p * 64 : (p + 1) * 64, lanes] = jnp.where(low_pair, value, 0.0).astype(BF)
+        packed_s[...] += dot_nt(left_s[...], right_s[...])
+        return counts
+
+    counts = lax.fori_loop(0, SOURCES // (STEP * LANES), pack, jnp.zeros((128, LANES), F32))
+    too_many = jnp.max(jnp.max(counts, axis=0, keepdims=True), axis=1, keepdims=True)
+    part = 0
+    for field, count in enumerate((3, 3, 2, 2, 1)):
+        value = packed_s[part * 64 : (part + 1) * 64, :]
+        for extra in range(1, count):
+            value = value + packed_s[(part + extra) * 64 : (part + extra + 1) * 64, :]
+        if field == 0:
+            value = jnp.where(too_many > RANKS, 4.0, value)
+        part += count
+        for half in range(2):
+            send_rec[pl.ds(half * 512 + field, 64, stride=8), :] = value[
+                :, half * LANES : (half + 1) * LANES
+            ]
+
+    pl.semaphore_wait(barrier, DEVICES - 1)
+
+    own_rec = pltpu.make_async_copy(
+        send_rec.at[pl.ds(pl.multiple_of(me * 8, 8), FIELDS)],
+        recv_rec.at[pl.ds(0, FIELDS)],
+        own_sem.at[0],
+    )
+    own_rec.start()
+    own_ph = pltpu.make_async_copy(
+        send_ph.at[:, pl.ds(pl.multiple_of(me * 4, 4), 4)],
+        recv_ph.at[:, pl.ds(pl.multiple_of(my_row * 4, 4), 4)],
+        own_sem.at[1],
+    )
+    own_ph.start()
+
+    def send_records(step, carry):
+        t = partner_at(step)
+        pltpu.make_async_remote_copy(
+            src_ref=send_rec.at[pl.ds(pl.multiple_of(t * 8, 8), FIELDS)],
+            dst_ref=recv_rec.at[pl.ds(pl.multiple_of(step * 8, 8), FIELDS)],
+            send_sem=rec_send,
+            recv_sem=rec_recv.at[step // GROUP],
+            device_id=device(t),
+            device_id_type=MESH,
+        ).start()
+        return carry
+
+    lax.fori_loop(1, DEVICES, send_records, 0)
+
+    for level in range(LEVELS):
+
+        def send_phases(step, carry):
+            t = partner_at(step)
+            pltpu.make_async_remote_copy(
+                src_ref=send_ph.at[level, pl.ds(pl.multiple_of(t * 4, 4), 4)],
+                dst_ref=recv_ph.at[level, pl.ds(pl.multiple_of(my_row * 4, 4), 4)],
+                send_sem=ph_send,
+                recv_sem=ph_recv.at[level],
+                device_id=device(t),
+                device_id_type=MESH,
+            ).start()
+            return carry
+
+        lax.fori_loop(1, DEVICES, send_phases, 0)
+
+    def wait_for(ref, rows, sem):
+        view = ref.at[pl.ds(0, rows)]
+        pltpu.make_async_copy(view, view, sem).wait()
+
+    leaf_s[...] = jnp.zeros_like(leaf_s)
+    own_rec.wait()
+
+    def add_group(group, rows, largest):
+        wait_for(recv_rec, rows, rec_recv.at[group])
+        first = group * (GROUP * 8)
+        if not isinstance(first, int):
+            first = pl.multiple_of(first, GROUP * 8)
+        field = [recv_rec[pl.ds(first + f, GROUP, stride=8), :] for f in range(FIELDS)]
+        for k, value in enumerate(basis_rows(field[1])):
+            basis_v[k * GROUP : (k + 1) * GROUP, :] = value
+        for k, value in enumerate(basis_rows(field[0])):
+            basis_c[k * GROUP : (k + 1) * GROUP, :] = value * field[2]
+            basis_s[k * GROUP : (k + 1) * GROUP, :] = value * field[3]
+        for s in range(GROUP):
+            lanes = slice(s * LANES, (s + 1) * LANES)
+            after = slice((GROUP + s) * LANES, (GROUP + s + 1) * LANES)
+            second = basis_v[pl.ds(s, Q, stride=GROUP), :]
+            for half, basis in enumerate((basis_c, basis_s)):
+                for i in range(Q):
+                    rows_i = slice(half * POINTS + i * Q, half * POINTS + (i + 1) * Q)
+                    term = basis[i * GROUP + s : i * GROUP + s + 1, :] * second
+                    high = term.astype(BF)
+                    terms_s[rows_i, lanes] = high
+                    terms_s[rows_i, after] = (term - high.astype(F32)).astype(BF)
+            hot_s[:, lanes] = jnp.where(row_256f == field[4][s : s + 1, :], 1.0, 0.0).astype(BF)
+        width = GROUP * LANES
+        leaf_s[...] += dot_nt(terms_s[:, :width], hot_s[...]) + dot_nt(
+            terms_s[:, width:], hot_s[...]
+        )
+        return jnp.maximum(largest, field[0])
+
+    largest = add_group(0, (GROUP - 1) * FIELDS, jnp.zeros((GROUP, LANES), F32))
+    largest = lax.fori_loop(
+        1, GROUPS, lambda group, seen: add_group(group, GROUP * FIELDS, seen), largest
+    )
+    flag[...] = largest
+    state_s[...] = leaf_s[...].T
+
+    own_ph.wait()
+    for level in range(LEVELS):
+        wait_for(recv_ph.at[level], (DEVICES - 1) * 4, ph_recv.at[level])
+        angle = jnp.concatenate(
+            [recv_ph[level, pl.ds(k, 256, stride=2), :] for k in range(2)], axis=1
+        )
+        cosine, sine = cos_sin(angle)
+        real, imag = state_s[:, :POINTS], state_s[:, POINTS:]
+        apart = 128 >> level
+        shape = (128 // apart, 2, apart, POINTS)
+        turned = [
+            (cosine * real - sine * imag).reshape(shape),
+            (sine * real + cosine * imag).reshape(shape),
+        ]
+        sides = [
+            jnp.concatenate([t[:, c].reshape(128, POINTS) for t in turned], axis=0)
+            for c in range(2)
+        ]
+        both = jnp.concatenate(sides, axis=1)
+        high = both.astype(BF)
+        low = (both - high.astype(F32)).astype(BF)
+        new = dot_nn(high, high_k[...]) + dot_nn(low, high_k[...]) + dot_nn(high, low_k[...])
+        for half in range(2):
+            part_new = new[half * 128 : (half + 1) * 128].reshape(128 // apart, 1, apart, POINTS)
+            state_s[:, half * POINTS : (half + 1) * POINTS] = jnp.broadcast_to(
+                part_new, shape
+            ).reshape(256, POINTS)
+
+    for k in range(4):
+        send_out[pl.ds(k, 256, stride=4), :] = state_s[:, k * LANES : (k + 1) * LANES]
+    own_out = pltpu.make_async_copy(
+        send_out.at[pl.ds(pl.multiple_of(my_row * 8, 8), 8)],
+        out.at[pl.ds(pl.multiple_of(me * 8, 8), 8)],
+        own_sem.at[2],
+    )
+    own_out.start()
+
+    def send_results(step, carry):
+        t = partner_at(step)
+        pltpu.make_async_remote_copy(
+            src_ref=send_out.at[pl.ds(pl.multiple_of(move_bits(t, ROW_BITS) * 8, 8), 8)],
+            dst_ref=out.at[pl.ds(pl.multiple_of(me * 8, 8), 8)],
+            send_sem=out_send,
+            recv_sem=out_recv,
+            device_id=device(t),
+            device_id_type=MESH,
+        ).start()
+        return carry
+
+    lax.fori_loop(1, DEVICES, send_results, 0)
+    own_out.wait()
+    wait_for(out, (DEVICES - 1) * 8, out_recv)
+    wait_for(send_rec, (DEVICES - 1) * FIELDS, rec_send)
+    for level in range(LEVELS):
+        wait_for(send_ph.at[level], (DEVICES - 1) * 4, ph_send)
+    wait_for(send_out, (DEVICES - 1) * 8, out_send)
+
+
+def fast(positions, angles, weights, owner_dev, leaf_slot, phase_table):
+    high_k, low_k = kron_table()
+    vmem = pl.BlockSpec(memory_space=pltpu.VMEM)
+    dma = pltpu.SemaphoreType.DMA
+    return pl.pallas_call(
+        body,
+        out_shape=(
+            jax.ShapeDtypeStruct((1024, LANES), F32),
+            jax.ShapeDtypeStruct((GROUP, LANES), F32),
+        ),
+        in_specs=[vmem] * 8,
+        out_specs=(vmem, vmem),
+        scratch_shapes=[
+            pltpu.VMEM((64, LANES), jnp.int32),
+            pltpu.VMEM((64, LANES), F32),
+            pltpu.VMEM((64, LANES), F32),
+            pltpu.VMEM((64, LANES), F32),
+            pltpu.VMEM((PARTS * 64, STEP * LANES), BF),
+            pltpu.VMEM((256, STEP * LANES), BF),
+            pltpu.VMEM((PARTS * 64, 256), F32),
+            pltpu.VMEM((1024, LANES), F32),
+            pltpu.VMEM((1024, LANES), F32),
+            pltpu.VMEM((LEVELS, 512, LANES), F32),
+            pltpu.VMEM((LEVELS, 512, LANES), F32),
+            pltpu.VMEM((1024, LANES), F32),
+            pltpu.VMEM((Q * GROUP, LANES), F32),
+            pltpu.VMEM((Q * GROUP, LANES), F32),
+            pltpu.VMEM((Q * GROUP, LANES), F32),
+            pltpu.VMEM((512, 2 * GROUP * LANES), BF),
+            pltpu.VMEM((256, GROUP * LANES), BF),
+            pltpu.VMEM((512, 256), F32),
+            pltpu.VMEM((256, 512), F32),
+            dma,
+            dma((GROUPS,)),
+            dma,
+            dma((LEVELS,)),
+            dma,
+            dma,
+            dma((3,)),
+        ],
+        compiler_params=pltpu.CompilerParams(
+            collective_id=0, has_side_effects=True, vmem_limit_bytes=48 << 20
+        ),
+    )(
+        positions,
+        angles.reshape(64, LANES),
+        weights.reshape(64, LANES),
+        owner_dev.reshape(64, LANES),
+        leaf_slot.reshape(64, LANES),
+        phase_table,
+        jnp.asarray(high_k),
+        jnp.asarray(low_k),
+    )
+
+
+def shards(*arrays):
+    result, largest = fast(*arrays)
+    return lax.cond(
+        jnp.max(largest) > 2.0, plain, lambda *_: result.reshape(256, 512), *arrays
+    )
+
+
 def solution(mesh):
     placed = (
         P(None, ("wide", "narrow")),

time: 741 us -> 67.6 us (0.09); the launches traced: 733 us -> 67.4 us
  local copies, waits for them, and re-layouts: 547 us -> 2.77 us
  Pallas kernels: 0 us -> 63.4 us
  other arithmetic: 63.9 us -> 0.6 us
  matrix products: 62.1 us -> 0 us
  waiting for transfers between devices: 30.5 us -> 0 us
  starting transfers between devices: 27.3 us -> 0 us
    gather x4 -> x0, local copies, waits for them, and re-layouts: 481 us -> none  [the longest x1 181 us: shards(): slot_source = jnp.take(source_order, slot_pick, axis=0)]
    pallas_call x0 -> x1, Pallas kernels: none -> 63.4 us  [fast(): pl.pallas_call(body, out_shape=(jax.ShapeDtypeStruct((1024, LANES), F32),...]
    dot_general x26 -> x0, matrix products: 62.1 us -> none  [the longest x16 48.3 us: add_block(): lax.dot_general(one_hot, term_rows, (((0,), (0,)), ((), ())), precision=H...]
    select_n x10 -> x0, local copies, waits for them, and re-layouts: 25.4 us -> none  [the longest x5 13.2 us: combine(): kron_own = jnp.where(side_bit == 1, kron_one, kron_zero)]
    rev x68 -> x0, local copies, waits for them, and re-layouts: 22 us -> none  [the longest x34 12.9 us: lagrange(): jnp.flip(offsets[..., 1:], -1)]
    all_to_all x2 -> x0, starting transfers between devices: 21.8 us -> none  [the longest x1 11.5 us: shards(): lax.all_to_all(index_send, ('wide', 'narrow'), split_axis=1, concat_axis=...]
    ppermute x5 -> x0, waiting for transfers between devices: 17.9 us -> none  [partner_2(): lax.ppermute(value, axis, [(i, i ^ 1 << apart) for i in range(lax.axis_si...]
    all_to_all x2 -> x0, waiting for transfers between devices: 12.7 us -> none  [the longest x1 12.6 us: shards(): lax.all_to_all(float_send, ('wide', 'narrow'), split_axis=1, concat_axis=...]
  transfers between devices with their start and end apart: 7 -> 0, of which waited for: 4 -> 0; matrix products, arithmetic and copies ran while one was open for 23% -> 0% of each run, Pallas kernels for 0% -> 0%
where the time goes in v1:
time: 67.6 us; the launch traced here: 67.4 us
  Pallas kernels  63.4 us (94%)
  local copies, waits for them, and re-layouts  2.77 us (4%)
    pallas_call x1, Pallas kernels, fast(): pl.pallas_call(body, out_shape=(jax.ShapeDtypeStruct((1024, LANES), F32),...  63.4 us
    unnamed x4, local copies, waits for them, and re-layouts  1.9 us

profile of v1, /device:TPU:1, one launch (start us, length us, event | category | flops | bytes accessed | tf_op | source)
XLA Modules:
  0.0 67.4 jit_solution(5939753822787772669)
XLA Ops:
  0.0 0.0 copy-start
  0.0 0.9 %copy-done = bf16[512,256]{1,0:T(8,128)(2,1)S(1)} copy-done((bf16[512,256]{1,0:T(8,128)(2,1)S(1)}, bf16[512,256]{1,0:T(8,128)(2,1)}, u32[]{:S(2)}) %copy-start) | copy-done | bytes 262168
  1.0 0.0 copy-start.1
  1.0 0.9 %copy-done.1 = bf16[512,256]{1,0:T(8,128)(2,1)S(1)} copy-done((bf16[512,256]{1,0:T(8,128)(2,1)S(1)}, bf16[512,256]{1,0:T(8,128)(2,1)}, u32[]{:S(2)}) %copy-start.1) | copy-done | bytes 262168
  1.9 63.4 %shard_map.84 = (f32[1024,128]{1,0:T(8,128)S(1)}, f32[8,128]{1,0:T(8,128)S(1)}) custom-call(f32[2,8192]{1,0:T(2,128)} %pos.1, f32[64,128]{1,0:T(8,128)} %bitcast.169, f32[64,128]{1,0:T(8,128)} %bitcast.171, s32[64,128]{1,0:T(8,128)} %bitcast.164, s32[64,128]{1,0:T(8,128)} %bitcast.153, f32[5,256,256]{2,1,0:T(8,128)} %phase.1, ...), custom_call_target="tpu_custom_call" | custom-call | tf_op jit(solution)/shard_map/pallas_call | solution.py:504
  65.3 0.6 reduce_max.9
  66.5 0.9 %conditional.1 = (f32[256,512]{1,0:T(8,128)}) conditional(s32[]{:T(128)} %convert_element_type.25, f32[1024,128]{1,0:T(8,128)S(1)} %get-tuple-element.180, (f32[5,256,256]{2,1,0:T(8,128)}, s32[8192,1]{0,1:T(1,128)}, f32[8192]{0:T(1024)}, f32[8192]{0:T(1024)}, f32[2,8192]{1,0:T(2,128)}, /*index=5*/s32[8192]{0:T(1024)}) %tuple.37), branch_computations={%region_1.0_spmd, %region_2.19_spmd} | conditional | flops 7263794176 | bytes 94257968 | solution.py:557
  66.6 0.9 %reshape.408 = f32[256,512]{1,0:T(8,128)} reshape(f32[1024,128]{1,0:T(8,128)S(1)} %param) | data formatting | bytes 1048576 | tf_op jit(solution)/shard_map/cond/branch_0_fun/reshape | solution.py:558
Async XLA Ops:
  0.0 0.9 %copy-start = (bf16[512,256]{1,0:T(8,128)(2,1)S(1)}, bf16[512,256]{1,0:T(8,128)(2,1)}, u32[]{:S(2)}) copy-start(bf16[512,256]{1,0:T(8,128)(2,1)} %constant.190.clone.low_k) | copy-start | bytes 786436
  1.0 0.9 %copy-start.1 = (bf16[512,256]{1,0:T(8,128)(2,1)S(1)}, bf16[512,256]{1,0:T(8,128)(2,1)}, u32[]{:S(2)}) copy-start(bf16[512,256]{1,0:T(8,128)(2,1)} %constant.189.clone.high_k) | copy-start | bytes 786436

commit v2 on v1

--- a/solution.py
+++ b/solution.py
@@ -251,6 +251,14 @@
     return out
 
 
+def move_bits_of(number, table):
+    return sum(((number >> source) & 1) << target for source, target in table)
+
+
+GROUP_BITS = tuple((step - 3, bit) for step, bit in STEP_BITS if step >= 3)
+GROUP_ROW_BITS = tuple((step, dict(ROW_BITS)[bit]) for step, bit in GROUP_BITS)
+
+
 def dot_nt(left, right):
     return lax.dot_general(left, right, (((1,), (1,)), ((), ())), preferred_element_type=F32)
 
@@ -260,11 +268,12 @@
 
 
 def body(
-    pos, ang, wgt, own, slot, phase, high_k, low_k,
+    pos_h, ang_h, wgt_h, own_h, slot_h, phase_h, high_h, low_h,
     out, flag,
+    pos, ang, wgt, own, slot, phase, high_k, low_k, load_sem,
     pair_s, box_s, wc_s, ws_s, left_s, right_s, packed_s,
     send_rec, recv_rec, send_ph, recv_ph, send_out,
-    basis_v, basis_c, basis_s, terms_s, hot_s, leaf_s, state_s,
+    basis_v, basis_c, basis_s, terms_a, terms_b, hot_a, hot_b, leaf_s, state_s,
     rec_send, rec_recv, ph_send, ph_recv, out_send, out_recv, own_sem,
 ):
     me = lax.axis_index("wide") * 8 + lax.axis_index("narrow")
@@ -273,18 +282,58 @@
     def device(t):
         return {"wide": lax.shift_right_logical(t, 3), "narrow": lax.bitwise_and(t, 7)}
 
-    def partner_at(step):
-        return lax.bitwise_xor(me, move_bits(step, STEP_BITS))
+    def for_partners(act):
+        def visit(group, first):
+            base = me if first else lax.bitwise_xor(me, move_bits(group, GROUP_BITS))
+            base_row = my_row if first else lax.bitwise_xor(my_row, move_bits(group, GROUP_ROW_BITS))
+            for j in range(1 if first else 0, GROUP):
+                offset = move_bits_of(j, STEP_BITS)
+                act(
+                    group,
+                    j,
+                    lax.bitwise_xor(base, offset),
+                    lax.bitwise_xor(base_row, move_bits_of(offset, ROW_BITS)),
+                )
+
+        visit(0, True)
+
+        def later(group, carry):
+            visit(group, False)
+            return carry
+
+        lax.fori_loop(1, GROUPS, later, 0)
+
+    loads = [
+        pltpu.make_async_copy(source, target, load_sem.at[i])
+        for i, (source, target) in enumerate(
+            (
+                (phase_h, phase),
+                (pos_h, pos),
+                (ang_h, ang),
+                (wgt_h, wgt),
+                (own_h, own),
+                (slot_h, slot),
+                (high_h, high_k),
+                (low_h, low_k),
+            )
+        )
+    ]
+    for load in loads:
+        load.start()
 
     barrier = pltpu.get_barrier_semaphore()
 
-    def greet(step, carry):
-        pl.semaphore_signal(
-            barrier, inc=1, device_id=device(partner_at(step)), device_id_type=MESH
-        )
-        return carry
-
-    lax.fori_loop(1, DEVICES, greet, 0)
+    def greet(group, j, t, row):
+        pl.semaphore_signal(barrier, inc=1, device_id=device(t), device_id_type=MESH)
+
+    for_partners(greet)
+
+    def rows_of(block, count):
+        first = block * 8
+        return pl.ds(first if isinstance(first, int) else pl.multiple_of(first, 8), count)
+
+    for load in loads[:6]:
+        load.wait()
 
     for level in range(LEVELS):
         for k in range(2):
@@ -366,24 +415,21 @@
     )
     own_ph.start()
 
-    def send_records(step, carry):
-        t = partner_at(step)
+    def send_records(group, j, t, row):
         pltpu.make_async_remote_copy(
             src_ref=send_rec.at[pl.ds(pl.multiple_of(t * 8, 8), FIELDS)],
-            dst_ref=recv_rec.at[pl.ds(pl.multiple_of(step * 8, 8), FIELDS)],
+            dst_ref=recv_rec.at[rows_of(group * GROUP + j, FIELDS)],
             send_sem=rec_send,
-            recv_sem=rec_recv.at[step // GROUP],
+            recv_sem=rec_recv.at[group],
             device_id=device(t),
             device_id_type=MESH,
         ).start()
-        return carry
-
-    lax.fori_loop(1, DEVICES, send_records, 0)
+
+    for_partners(send_records)
 
     for level in range(LEVELS):
 
-        def send_phases(step, carry):
-            t = partner_at(step)
+        def send_phases(group, j, t, row):
             pltpu.make_async_remote_copy(
                 src_ref=send_ph.at[level, pl.ds(pl.multiple_of(t * 4, 4), 4)],
                 dst_ref=recv_ph.at[level, pl.ds(pl.multiple_of(my_row * 4, 4), 4)],
@@ -392,9 +438,8 @@
                 device_id=device(t),
                 device_id_type=MESH,
             ).start()
-            return carry
-
-        lax.fori_loop(1, DEVICES, send_phases, 0)
+
+        for_partners(send_phases)
 
     def wait_for(ref, rows, sem):
         view = ref.at[pl.ds(0, rows)]
@@ -403,8 +448,10 @@
     leaf_s[...] = jnp.zeros_like(leaf_s)
     own_rec.wait()
 
-    def add_group(group, rows, largest):
-        wait_for(recv_rec, rows, rec_recv.at[group])
+    def arrived(group):
+        wait_for(recv_rec, GROUP * FIELDS, rec_recv.at[group])
+
+    def build(group, terms, hot, largest):
         first = group * (GROUP * 8)
         if not isinstance(first, int):
             first = pl.multiple_of(first, GROUP * 8)
@@ -423,20 +470,36 @@
                     rows_i = slice(half * POINTS + i * Q, half * POINTS + (i + 1) * Q)
                     term = basis[i * GROUP + s : i * GROUP + s + 1, :] * second
                     high = term.astype(BF)
-                    terms_s[rows_i, lanes] = high
-                    terms_s[rows_i, after] = (term - high.astype(F32)).astype(BF)
-            hot_s[:, lanes] = jnp.where(row_256f == field[4][s : s + 1, :], 1.0, 0.0).astype(BF)
-        width = GROUP * LANES
-        leaf_s[...] += dot_nt(terms_s[:, :width], hot_s[...]) + dot_nt(
-            terms_s[:, width:], hot_s[...]
-        )
+                    terms[rows_i, lanes] = high
+                    terms[rows_i, after] = (term - high.astype(F32)).astype(BF)
+            named = jnp.where(row_256f == field[4][s : s + 1, :], 1.0, 0.0).astype(BF)
+            hot[:, lanes] = named
+            hot[:, after] = named
         return jnp.maximum(largest, field[0])
 
-    largest = add_group(0, (GROUP - 1) * FIELDS, jnp.zeros((GROUP, LANES), F32))
-    largest = lax.fori_loop(
-        1, GROUPS, lambda group, seen: add_group(group, GROUP * FIELDS, seen), largest
-    )
-    flag[...] = largest
+    def add(terms, hot):
+        leaf_s[...] += dot_nt(terms[...], hot[...])
+
+    wait_for(recv_rec, (GROUP - 1) * FIELDS, rec_recv.at[0])
+    largest = build(0, terms_a, hot_a, jnp.zeros((GROUP, LANES), F32))
+
+    def two_groups(pair, largest):
+        arrived(2 * pair + 1)
+        arrived(2 * pair + 2)
+        largest = build(2 * pair + 1, terms_b, hot_b, largest)
+        add(terms_a, hot_a)
+        largest = build(2 * pair + 2, terms_a, hot_a, largest)
+        add(terms_b, hot_b)
+        return largest
+
+    largest = lax.fori_loop(0, GROUPS // 2 - 1, two_groups, largest)
+    arrived(GROUPS - 1)
+    largest = build(GROUPS - 1, terms_b, hot_b, largest)
+    add(terms_a, hot_a)
+    add(terms_b, hot_b)
+    flag[0, 0] = jnp.max(largest)
+    for load in loads[6:]:
+        load.wait()
     state_s[...] = leaf_s[...].T
 
     own_ph.wait()
@@ -476,19 +539,17 @@
     )
     own_out.start()
 
-    def send_results(step, carry):
-        t = partner_at(step)
+    def send_results(group, j, t, row):
         pltpu.make_async_remote_copy(
-            src_ref=send_out.at[pl.ds(pl.multiple_of(move_bits(t, ROW_BITS) * 8, 8), 8)],
+            src_ref=send_out.at[rows_of(row, 8)],
             dst_ref=out.at[pl.ds(pl.multiple_of(me * 8, 8), 8)],
             send_sem=out_send,
             recv_sem=out_recv,
             device_id=device(t),
             device_id_type=MESH,
         ).start()
-        return carry
-
-    lax.fori_loop(1, DEVICES, send_results, 0)
+
+    for_partners(send_results)
     own_out.wait()
     wait_for(out, (DEVICES - 1) * 8, out_recv)
     wait_for(send_rec, (DEVICES - 1) * FIELDS, rec_send)
@@ -499,17 +560,28 @@
 
 def fast(positions, angles, weights, owner_dev, leaf_slot, phase_table):
     high_k, low_k = kron_table()
-    vmem = pl.BlockSpec(memory_space=pltpu.VMEM)
     dma = pltpu.SemaphoreType.DMA
     return pl.pallas_call(
         body,
         out_shape=(
             jax.ShapeDtypeStruct((1024, LANES), F32),
-            jax.ShapeDtypeStruct((GROUP, LANES), F32),
+            jax.ShapeDtypeStruct((1, 1), F32),
         ),
-        in_specs=[vmem] * 8,
-        out_specs=(vmem, vmem),
+        in_specs=[pl.BlockSpec(memory_space=pl.ANY)] * 8,
+        out_specs=(
+            pl.BlockSpec(memory_space=pl.ANY),
+            pl.BlockSpec(memory_space=pltpu.SMEM),
+        ),
         scratch_shapes=[
+            pltpu.VMEM((2, SOURCES), F32),
+            pltpu.VMEM((64, LANES), F32),
+            pltpu.VMEM((64, LANES), F32),
+            pltpu.VMEM((64, LANES), jnp.int32),
+            pltpu.VMEM((64, LANES), jnp.int32),
+            pltpu.VMEM((LEVELS, 256, POINTS), F32),
+            pltpu.VMEM((512, POINTS), BF),
+            pltpu.VMEM((512, POINTS), BF),
+            dma((8,)),
             pltpu.VMEM((64, LANES), jnp.int32),
             pltpu.VMEM((64, LANES), F32),
             pltpu.VMEM((64, LANES), F32),
@@ -526,7 +598,9 @@
             pltpu.VMEM((Q * GROUP, LANES), F32),
             pltpu.VMEM((Q * GROUP, LANES), F32),
             pltpu.VMEM((512, 2 * GROUP * LANES), BF),
-            pltpu.VMEM((256, GROUP * LANES), BF),
+            pltpu.VMEM((512, 2 * GROUP * LANES), BF),
+            pltpu.VMEM((256, 2 * GROUP * LANES), BF),
+            pltpu.VMEM((256, 2 * GROUP * LANES), BF),
             pltpu.VMEM((512, 256), F32),
             pltpu.VMEM((256, 512), F32),
             dma,
@@ -538,7 +612,7 @@
             dma((3,)),
         ],
         compiler_params=pltpu.CompilerParams(
-            collective_id=0, has_side_effects=True, vmem_limit_bytes=48 << 20
+            collective_id=0, has_side_effects=True, vmem_limit_bytes=56 << 20
         ),
     )(
         positions,
@@ -555,7 +629,7 @@
 def shards(*arrays):
     result, largest = fast(*arrays)
     return lax.cond(
-        jnp.max(largest) > 2.0, plain, lambda *_: result.reshape(256, 512), *arrays
+        largest[0, 0] > 2.0, plain, lambda *_: result.reshape(256, 512), *arrays
     )
 
 

time: 67.6 us -> 58.6 us (0.87)
  Pallas kernels: 63.4 us -> 56.7 us
  local copies, waits for them, and re-layouts: 2.77 us -> 0.87 us
    pallas_call x1, Pallas kernels: 63.4 us -> 56.7 us  [fast(): pl.pallas_call(body, out_shape=(jax.ShapeDtypeStruct((1024, LANES), F32),...]
    unnamed x4 -> x2, local copies, waits for them, and re-layouts: 1.9 us -> 0.79 us
    reshape x1, local copies, waits for them, and re-layouts: 0.87 us -> 0.08 us  [shards(): result.reshape(256, 512)]
where the time goes in v2:
time: 58.6 us; the launch traced here: 58.5 us
  Pallas kernels  56.7 us (97%)
  local copies, waits for them, and re-layouts  0.87 us (1%)
  between operations  0.72 us (1%)
    pallas_call x1, Pallas kernels, fast(): pl.pallas_call(body, out_shape=(jax.ShapeDtypeStruct((1024, LANES), F32),...  56.7 us

profile of v2, /device:TPU:1, one launch (start us, length us, event | category | flops | bytes accessed | tf_op | source)
XLA Modules:
  0.0 58.5 jit_solution(16155742300631725149)
XLA Ops:
  0.0 56.7 %shard_map.84 = (f32[1024,128]{1,0:T(8,128)S(1)}, f32[1,1]{1,0:T(1,128)}) custom-call(f32[2,8192]{1,0:T(2,128)} %pos_h.1, f32[64,128]{1,0:T(8,128)} %bitcast.170, f32[64,128]{1,0:T(8,128)} %bitcast.172, s32[64,128]{1,0:T(8,128)} %bitcast.165, s32[64,128]{1,0:T(8,128)} %bitcast.154, f32[5,256,256]{2,1,0:T(8,128)} %phase_h.1, ...), custom_call_target="tpu_custom_call" | custom-call | tf_op jit(solution)/shard_map/pallas_call | solution.py:564
  57.4 0.3 conditional.1
  57.4 0.1 reshape.412
  57.7 0.0 copy-start.2
  57.7 0.8 %copy-done.2 = f32[256,512]{1,0:T(8,128)} copy-done((f32[256,512]{1,0:T(8,128)}, f32[256,512]{1,0:T(8,128)S(1)}, u32[]{:S(2)}) %copy-start.2) | copy-done | bytes 524312
Async XLA Ops:
  57.7 0.8 %copy-start.2 = (f32[256,512]{1,0:T(8,128)}, f32[256,512]{1,0:T(8,128)S(1)}, u32[]{:S(2)}) copy-start(f32[256,512]{1,0:T(8,128)S(1)} %get-tuple-element.370) | copy-start | bytes 1572868

commit v3 on v2

--- a/solution.py
+++ b/solution.py
@@ -27,6 +27,9 @@
 STEP = 8
 GROUP = 8
 GROUPS = DEVICES // GROUP
+BLOCKS = SOURCES // (STEP * LANES)
+EARLY = 3
+BATCHES = (slice(0, 3), slice(3, 5))
 ROW_BITS = ((0, 6), (1, 5), (3, 4), (4, 3), (6, 2), (2, 1), (5, 0))
 STEP_BITS = ((6, 6), (5, 2), (4, 0), (3, 5), (2, 1), (1, 4), (0, 3))
 BF = jnp.bfloat16
@@ -271,9 +274,9 @@
     pos_h, ang_h, wgt_h, own_h, slot_h, phase_h, high_h, low_h,
     out, flag,
     pos, ang, wgt, own, slot, phase, high_k, low_k, load_sem,
-    pair_s, box_s, wc_s, ws_s, left_s, right_s, packed_s,
+    pair_s, box_s, wc_s, ws_s, left_a, left_b, right_a, right_b, packed_s,
     send_rec, recv_rec, send_ph, recv_ph, send_out,
-    basis_v, basis_c, basis_s, terms_a, terms_b, hot_a, hot_b, leaf_s, state_s,
+    basis_v, basis_c, basis_s, terms_s, hot_s, leaf_s, state_s, angle_s,
     rec_send, rec_recv, ph_send, ph_recv, out_send, out_recv, own_sem,
 ):
     me = lax.axis_index("wide") * 8 + lax.axis_index("narrow")
@@ -357,7 +360,7 @@
     column = lax.broadcasted_iota(jnp.int32, (LANES, 256), 1)
     counter = jnp.where((before < column) | (column >= LANES), 1.0, 0.0).astype(BF)
 
-    def pack(block, counts):
+    def lay_out(block, left, right, counts):
         for j in range(STEP):
             c = block * STEP + j
             lanes = slice(j * LANES, (j + 1) * LANES)
@@ -370,7 +373,7 @@
             counts = counts + seen[:, LANES:]
             high_pair = lax.shift_right_logical(pair, 6).astype(F32) * RANKS
             place = jnp.where(rank < RANKS, high_pair + rank, -1.0)
-            right_s[:, lanes] = jnp.where(row_256f == place, 1.0, 0.0).astype(BF)
+            right[:, lanes] = jnp.where(row_256f == place, 1.0, 0.0).astype(BF)
             low_pair = row_64 == lax.bitwise_and(pair, 63)
             start = pl.multiple_of(c * LANES, LANES)
             values = (
@@ -381,11 +384,23 @@
                 + [box_s[pl.ds(c, 1), :]]
             )
             for p, value in enumerate(values):
-                left_s[p * 64 : (p + 1) * 64, lanes] = jnp.where(low_pair, value, 0.0).astype(BF)
-        packed_s[...] += dot_nt(left_s[...], right_s[...])
+                left[p * 64 : (p + 1) * 64, lanes] = jnp.where(low_pair, value, 0.0).astype(BF)
         return counts
 
-    counts = lax.fori_loop(0, SOURCES // (STEP * LANES), pack, jnp.zeros((128, LANES), F32))
+    def gather(left, right):
+        packed_s[...] += dot_nt(left[...], right[...])
+
+    def two_blocks(pair, counts):
+        counts = lay_out(2 * pair, left_a, right_a, counts)
+        gather(left_b, right_b)
+        counts = lay_out(2 * pair + 1, left_b, right_b, counts)
+        gather(left_a, right_a)
+        return counts
+
+    left_b[...] = jnp.zeros_like(left_b)
+    right_b[...] = jnp.zeros_like(right_b)
+    counts = lax.fori_loop(0, BLOCKS // 2, two_blocks, jnp.zeros((128, LANES), F32))
+    gather(left_b, right_b)
     too_many = jnp.max(jnp.max(counts, axis=0, keepdims=True), axis=1, keepdims=True)
     part = 0
     for field, count in enumerate((3, 3, 2, 2, 1)):
@@ -405,13 +420,13 @@
     own_rec = pltpu.make_async_copy(
         send_rec.at[pl.ds(pl.multiple_of(me * 8, 8), FIELDS)],
         recv_rec.at[pl.ds(0, FIELDS)],
-        own_sem.at[0],
+        rec_recv.at[0],
     )
     own_rec.start()
     own_ph = pltpu.make_async_copy(
         send_ph.at[:, pl.ds(pl.multiple_of(me * 4, 4), 4)],
         recv_ph.at[:, pl.ds(pl.multiple_of(my_row * 4, 4), 4)],
-        own_sem.at[1],
+        own_sem.at[0],
     )
     own_ph.start()
 
@@ -427,34 +442,35 @@
 
     for_partners(send_records)
 
-    for level in range(LEVELS):
-
-        def send_phases(group, j, t, row):
+    def send_phases(batch):
+        levels = BATCHES[batch]
+
+        def send(group, j, t, row):
             pltpu.make_async_remote_copy(
-                src_ref=send_ph.at[level, pl.ds(pl.multiple_of(t * 4, 4), 4)],
-                dst_ref=recv_ph.at[level, pl.ds(pl.multiple_of(my_row * 4, 4), 4)],
-                send_sem=ph_send,
-                recv_sem=ph_recv.at[level],
+                src_ref=send_ph.at[levels, pl.ds(pl.multiple_of(t * 4, 4), 4)],
+                dst_ref=recv_ph.at[levels, pl.ds(pl.multiple_of(my_row * 4, 4), 4)],
+                send_sem=ph_send.at[batch],
+                recv_sem=ph_recv.at[batch],
                 device_id=device(t),
                 device_id_type=MESH,
             ).start()
 
-        for_partners(send_phases)
+        for_partners(send)
+
+    send_phases(0)
 
     def wait_for(ref, rows, sem):
         view = ref.at[pl.ds(0, rows)]
         pltpu.make_async_copy(view, view, sem).wait()
 
+    def wait_phases(ref, batch, sems):
+        view = ref.at[BATCHES[batch], pl.ds(0, (DEVICES - 1) * 4)]
+        pltpu.make_async_copy(view, view, sems.at[batch]).wait()
+
     leaf_s[...] = jnp.zeros_like(leaf_s)
-    own_rec.wait()
-
-    def arrived(group):
-        wait_for(recv_rec, GROUP * FIELDS, rec_recv.at[group])
 
     def build(group, terms, hot, largest):
-        first = group * (GROUP * 8)
-        if not isinstance(first, int):
-            first = pl.multiple_of(first, GROUP * 8)
+        first = pl.multiple_of(group * (GROUP * 8), GROUP * 8)
         field = [recv_rec[pl.ds(first + f, GROUP, stride=8), :] for f in range(FIELDS)]
         for k, value in enumerate(basis_rows(field[1])):
             basis_v[k * GROUP : (k + 1) * GROUP, :] = value
@@ -477,65 +493,67 @@
             hot[:, after] = named
         return jnp.maximum(largest, field[0])
 
-    def add(terms, hot):
-        leaf_s[...] += dot_nt(terms[...], hot[...])
-
-    wait_for(recv_rec, (GROUP - 1) * FIELDS, rec_recv.at[0])
-    largest = build(0, terms_a, hot_a, jnp.zeros((GROUP, LANES), F32))
-
-    def two_groups(pair, largest):
-        arrived(2 * pair + 1)
-        arrived(2 * pair + 2)
-        largest = build(2 * pair + 1, terms_b, hot_b, largest)
-        add(terms_a, hot_a)
-        largest = build(2 * pair + 2, terms_a, hot_a, largest)
-        add(terms_b, hot_b)
+    def one_group(group, largest):
+        @pl.when(group == EARLY)
+        def _():
+            send_phases(1)
+
+        wait_for(recv_rec, GROUP * FIELDS, rec_recv.at[group])
+        largest = build(group, terms_s, hot_s, largest)
+        leaf_s[...] += dot_nt(terms_s[...], hot_s[...])
         return largest
 
-    largest = lax.fori_loop(0, GROUPS // 2 - 1, two_groups, largest)
-    arrived(GROUPS - 1)
-    largest = build(GROUPS - 1, terms_b, hot_b, largest)
-    add(terms_a, hot_a)
-    add(terms_b, hot_b)
+    largest = lax.fori_loop(0, GROUPS, one_group, jnp.zeros((GROUP, LANES), F32))
     flag[0, 0] = jnp.max(largest)
     for load in loads[6:]:
         load.wait()
     state_s[...] = leaf_s[...].T
 
     own_ph.wait()
-    for level in range(LEVELS):
-        wait_for(recv_ph.at[level], (DEVICES - 1) * 4, ph_recv.at[level])
-        angle = jnp.concatenate(
-            [recv_ph[level, pl.ds(k, 256, stride=2), :] for k in range(2)], axis=1
-        )
-        cosine, sine = cos_sin(angle)
+
+    def one_level(level, carry):
+        for batch, levels in enumerate(BATCHES):
+
+            @pl.when(level == levels.start)
+            def _():
+                wait_phases(recv_ph, batch, ph_recv)
+
+        for tile in range(32):
+            turned = lax.bitwise_and(
+                lax.bitwise_or(
+                    lax.shift_right_logical(jnp.int32(tile), level),
+                    lax.shift_left(jnp.int32(tile), LEVELS - level),
+                ),
+                31,
+            )
+            for k in range(2):
+                angle_s[tile * 8 : (tile + 1) * 8, k * LANES : (k + 1) * LANES] = recv_ph[
+                    level, pl.ds(turned * 16 + k, 8, stride=2), :
+                ]
+        cosine, sine = cos_sin(angle_s[...])
         real, imag = state_s[:, :POINTS], state_s[:, POINTS:]
-        apart = 128 >> level
-        shape = (128 // apart, 2, apart, POINTS)
-        turned = [
-            (cosine * real - sine * imag).reshape(shape),
-            (sine * real + cosine * imag).reshape(shape),
-        ]
-        sides = [
-            jnp.concatenate([t[:, c].reshape(128, POINTS) for t in turned], axis=0)
-            for c in range(2)
-        ]
-        both = jnp.concatenate(sides, axis=1)
+        both = []
+        for value in (cosine * real - sine * imag, sine * real + cosine * imag):
+            both.append(jnp.concatenate([value[:128], value[128:]], axis=1))
+        both = jnp.concatenate(both, axis=0)
         high = both.astype(BF)
         low = (both - high.astype(F32)).astype(BF)
         new = dot_nn(high, high_k[...]) + dot_nn(low, high_k[...]) + dot_nn(high, low_k[...])
         for half in range(2):
-            part_new = new[half * 128 : (half + 1) * 128].reshape(128 // apart, 1, apart, POINTS)
+            part_new = new[half * 128 : (half + 1) * 128].reshape(16, 1, 8, POINTS)
             state_s[:, half * POINTS : (half + 1) * POINTS] = jnp.broadcast_to(
-                part_new, shape
+                part_new, (16, 2, 8, POINTS)
             ).reshape(256, POINTS)
+        return carry
+
+    lax.fori_loop(0, LEVELS, one_level, 0)
 
     for k in range(4):
         send_out[pl.ds(k, 256, stride=4), :] = state_s[:, k * LANES : (k + 1) * LANES]
     own_out = pltpu.make_async_copy(
         send_out.at[pl.ds(pl.multiple_of(my_row * 8, 8), 8)],
         out.at[pl.ds(pl.multiple_of(me * 8, 8), 8)],
-        own_sem.at[2],
+        own_sem.at[1],
     )
     own_out.start()
 
@@ -553,8 +571,8 @@
     own_out.wait()
     wait_for(out, (DEVICES - 1) * 8, out_recv)
     wait_for(send_rec, (DEVICES - 1) * FIELDS, rec_send)
-    for level in range(LEVELS):
-        wait_for(send_ph.at[level], (DEVICES - 1) * 4, ph_send)
+    for batch in range(len(BATCHES)):
+        wait_phases(send_ph, batch, ph_send)
     wait_for(send_out, (DEVICES - 1) * 8, out_send)
 
 
@@ -587,6 +605,8 @@
             pltpu.VMEM((64, LANES), F32),
             pltpu.VMEM((64, LANES), F32),
             pltpu.VMEM((PARTS * 64, STEP * LANES), BF),
+            pltpu.VMEM((PARTS * 64, STEP * LANES), BF),
+            pltpu.VMEM((256, STEP * LANES), BF),
             pltpu.VMEM((256, STEP * LANES), BF),
             pltpu.VMEM((PARTS * 64, 256), F32),
             pltpu.VMEM((1024, LANES), F32),
@@ -598,18 +618,17 @@
             pltpu.VMEM((Q * GROUP, LANES), F32),
             pltpu.VMEM((Q * GROUP, LANES), F32),
             pltpu.VMEM((512, 2 * GROUP * LANES), BF),
-            pltpu.VMEM((512, 2 * GROUP * LANES), BF),
-            pltpu.VMEM((256, 2 * GROUP * LANES), BF),
             pltpu.VMEM((256, 2 * GROUP * LANES), BF),
             pltpu.VMEM((512, 256), F32),
             pltpu.VMEM((256, 512), F32),
+            pltpu.VMEM((256, POINTS), F32),
             dma,
             dma((GROUPS,)),
-            dma,
-            dma((LEVELS,)),
+            dma((len(BATCHES),)),
+            dma((len(BATCHES),)),
             dma,
             dma,
-            dma((3,)),
+            dma((2,)),
         ],
         compiler_params=pltpu.CompilerParams(
             collective_id=0, has_side_effects=True, vmem_limit_bytes=56 << 20

time: 58.6 us -> 55.2 us (0.942)
  Pallas kernels: 56.7 us -> 53.2 us
    pallas_call x1, Pallas kernels: 56.7 us -> 53.2 us  [fast(): pl.pallas_call(body, out_shape=(jax.ShapeDtypeStruct((1024, LANES), F32),...]
where the time goes in v3:
time: 55.2 us; the launch traced here: 55 us
  Pallas kernels  53.2 us (96%)
  local copies, waits for them, and re-layouts  0.87 us (2%)
  between operations  0.72 us (1%)
    pallas_call x1, Pallas kernels, fast(): pl.pallas_call(body, out_shape=(jax.ShapeDtypeStruct((1024, LANES), F32),...  53.2 us

profile of v3, /device:TPU:1, one launch (start us, length us, event | category | flops | bytes accessed | tf_op | source)
XLA Modules:
  0.0 55.0 jit_solution(6982654350862714842)
XLA Ops:
  0.0 53.2 %shard_map.84 = (f32[1024,128]{1,0:T(8,128)S(1)}, f32[1,1]{1,0:T(1,128)}) custom-call(f32[2,8192]{1,0:T(2,128)} %pos_h.1, f32[64,128]{1,0:T(8,128)} %bitcast.170, f32[64,128]{1,0:T(8,128)} %bitcast.172, s32[64,128]{1,0:T(8,128)} %bitcast.165, s32[64,128]{1,0:T(8,128)} %bitcast.154, f32[5,256,256]{2,1,0:T(8,128)} %phase_h.1, ...), custom_call_target="tpu_custom_call" | custom-call | tf_op jit(solution)/shard_map/pallas_call | solution.py:582
  53.9 0.3 conditional.1
  53.9 0.1 reshape.412
  54.3 0.0 copy-start.2
  54.3 0.8 %copy-done.2 = f32[256,512]{1,0:T(8,128)} copy-done((f32[256,512]{1,0:T(8,128)}, f32[256,512]{1,0:T(8,128)S(1)}, u32[]{:S(2)}) %copy-start.2) | copy-done | bytes 524312
Async XLA Ops:
  54.3 0.8 %copy-start.2 = (f32[256,512]{1,0:T(8,128)}, f32[256,512]{1,0:T(8,128)S(1)}, u32[]{:S(2)}) copy-start(f32[256,512]{1,0:T(8,128)S(1)} %get-tuple-element.370) | copy-start | bytes 1572868

commit v4 on v3

--- a/solution.py
+++ b/solution.py
@@ -28,8 +28,7 @@
 GROUP = 8
 GROUPS = DEVICES // GROUP
 BLOCKS = SOURCES // (STEP * LANES)
-EARLY = 3
-BATCHES = (slice(0, 3), slice(3, 5))
+BATCHES = (slice(0, 5),)
 ROW_BITS = ((0, 6), (1, 5), (3, 4), (4, 3), (6, 2), (2, 1), (5, 0))
 STEP_BITS = ((6, 6), (5, 2), (4, 0), (3, 5), (2, 1), (1, 4), (0, 3))
 BF = jnp.bfloat16
@@ -188,7 +187,7 @@
     table = np.concatenate(blocks, 0) * SQRT_HALF
     high = table.astype(np.float32).astype(BF)
     low = (table - high.astype(np.float64)).astype(np.float32).astype(BF)
-    return high, low
+    return np.concatenate([high, high, low], 0)
 
 
 def series(function, degree):
@@ -198,8 +197,8 @@
     return [float(c) for c in fit.convert(kind=np.polynomial.Polynomial).coef]
 
 
-COS_SERIES = series(np.cos, 7)
-SIN_SERIES = series(lambda x: np.sinc(x / np.pi), 7)
+COS_SERIES = series(np.cos, 6)
+SIN_SERIES = series(lambda x: np.sinc(x / np.pi), 6)
 
 
 def cos_sin(angle):
@@ -271,9 +270,9 @@
 
 
 def body(
-    pos_h, ang_h, wgt_h, own_h, slot_h, phase_h, high_h, low_h,
+    pos_h, ang_h, wgt_h, own_h, slot_h, phase_h, all_h,
     out, flag,
-    pos, ang, wgt, own, slot, phase, high_k, low_k, load_sem,
+    pos, ang, wgt, own, slot, phase, all_k, load_sem,
     pair_s, box_s, wc_s, ws_s, left_a, left_b, right_a, right_b, packed_s,
     send_rec, recv_rec, send_ph, recv_ph, send_out,
     basis_v, basis_c, basis_s, terms_s, hot_s, leaf_s, state_s, angle_s,
@@ -316,8 +315,7 @@
                 (wgt_h, wgt),
                 (own_h, own),
                 (slot_h, slot),
-                (high_h, high_k),
-                (low_h, low_k),
+                (all_h, all_k),
             )
         )
     ]
@@ -335,12 +333,8 @@
         first = block * 8
         return pl.ds(first if isinstance(first, int) else pl.multiple_of(first, 8), count)
 
-    for load in loads[:6]:
+    for load in loads[1:6]:
         load.wait()
-
-    for level in range(LEVELS):
-        for k in range(2):
-            send_ph[level, pl.ds(k, 256, stride=2), :] = phase[level, :, k * LANES : (k + 1) * LANES]
 
     slots = slot[...]
     pair_s[...] = lax.shift_right_logical(slots, 1)
@@ -423,13 +417,6 @@
         rec_recv.at[0],
     )
     own_rec.start()
-    own_ph = pltpu.make_async_copy(
-        send_ph.at[:, pl.ds(pl.multiple_of(me * 4, 4), 4)],
-        recv_ph.at[:, pl.ds(pl.multiple_of(my_row * 4, 4), 4)],
-        own_sem.at[0],
-    )
-    own_ph.start()
-
     def send_records(group, j, t, row):
         pltpu.make_async_remote_copy(
             src_ref=send_rec.at[pl.ds(pl.multiple_of(t * 8, 8), FIELDS)],
@@ -457,6 +444,17 @@
 
         for_partners(send)
 
+    loads[0].wait()
+    for level in range(LEVELS):
+        for k in range(2):
+            send_ph[level, pl.ds(k, 256, stride=2), :] = phase[level, :, k * LANES : (k + 1) * LANES]
+
+    own_ph = pltpu.make_async_copy(
+        send_ph.at[:, pl.ds(pl.multiple_of(me * 4, 4), 4)],
+        recv_ph.at[:, pl.ds(pl.multiple_of(my_row * 4, 4), 4)],
+        own_sem.at[0],
+    )
+    own_ph.start()
     send_phases(0)
 
     def wait_for(ref, rows, sem):
@@ -494,10 +492,6 @@
         return jnp.maximum(largest, field[0])
 
     def one_group(group, largest):
-        @pl.when(group == EARLY)
-        def _():
-            send_phases(1)
-
         wait_for(recv_rec, GROUP * FIELDS, rec_recv.at[group])
         largest = build(group, terms_s, hot_s, largest)
         leaf_s[...] += dot_nt(terms_s[...], hot_s[...])
@@ -538,7 +532,7 @@
         both = jnp.concatenate(both, axis=0)
         high = both.astype(BF)
         low = (both - high.astype(F32)).astype(BF)
-        new = dot_nn(high, high_k[...]) + dot_nn(low, high_k[...]) + dot_nn(high, low_k[...])
+        new = dot_nn(jnp.concatenate([high, low, high], axis=1), all_k[...])
         for half in range(2):
             part_new = new[half * 128 : (half + 1) * 128].reshape(16, 1, 8, POINTS)
             state_s[:, half * POINTS : (half + 1) * POINTS] = jnp.broadcast_to(
@@ -577,7 +571,6 @@
 
 
 def fast(positions, angles, weights, owner_dev, leaf_slot, phase_table):
-    high_k, low_k = kron_table()
     dma = pltpu.SemaphoreType.DMA
     return pl.pallas_call(
         body,
@@ -585,7 +578,7 @@
             jax.ShapeDtypeStruct((1024, LANES), F32),
             jax.ShapeDtypeStruct((1, 1), F32),
         ),
-        in_specs=[pl.BlockSpec(memory_space=pl.ANY)] * 8,
+        in_specs=[pl.BlockSpec(memory_space=pl.ANY)] * 7,
         out_specs=(
             pl.BlockSpec(memory_space=pl.ANY),
             pl.BlockSpec(memory_space=pltpu.SMEM),
@@ -597,9 +590,8 @@
             pltpu.VMEM((64, LANES), jnp.int32),
             pltpu.VMEM((64, LANES), jnp.int32),
             pltpu.VMEM((LEVELS, 256, POINTS), F32),
-            pltpu.VMEM((512, POINTS), BF),
-            pltpu.VMEM((512, POINTS), BF),
-            dma((8,)),
+            pltpu.VMEM((1536, POINTS), BF),
+            dma((7,)),
             pltpu.VMEM((64, LANES), jnp.int32),
             pltpu.VMEM((64, LANES), F32),
             pltpu.VMEM((64, LANES), F32),
@@ -640,8 +632,7 @@
         owner_dev.reshape(64, LANES),
         leaf_slot.reshape(64, LANES),
         phase_table,
-        jnp.asarray(high_k),
-        jnp.asarray(low_k),
+        jnp.asarray(kron_table()),
     )
 
 

time: 55.2 us -> 53.6 us (0.971)
  Pallas kernels: 53.2 us -> 51.8 us
    pallas_call x1, Pallas kernels: 53.2 us -> 51.8 us  [fast(): pl.pallas_call(body, out_shape=(jax.ShapeDtypeStruct((1024, LANES), F32),...]
    reshape x1, local copies, waits for them, and re-layouts: 0.08 us -> 0.87 us  [shards(): result.reshape(256, 512)]
    unnamed x2 -> x12, local copies, waits for them, and re-layouts: 0.79 us -> 0.02 us
where the time goes in v4:
time: 53.6 us; the launch traced here: 53.5 us
  Pallas kernels  51.8 us (97%)
  local copies, waits for them, and re-layouts  0.9 us (2%)
  between operations  0.78 us (1%)
    pallas_call x1, Pallas kernels, fast(): pl.pallas_call(body, out_shape=(jax.ShapeDtypeStruct((1024, LANES), F32),...  51.8 us

profile of v4, /device:TPU:1, one launch (start us, length us, event | category | flops | bytes accessed | tf_op | source)
XLA Modules:
  0.0 53.5 jit_solution(837081500462128052)
XLA Ops:
  0.0 0.0 copy-start.1
  0.0 0.0 copy-start
  0.0 0.0 copy-start.2
  0.0 0.0 copy-start.5
  0.0 0.0 copy-start.4
  0.0 0.0 copy-start.3
  0.0 51.8 %shard_map.75 = (f32[1024,128]{1,0:T(8,128)S(1)}, f32[1,1]{1,0:T(1,128)}) custom-call(f32[2,8192]{1,0:T(2,128)} %pos_h.1, f32[64,128]{1,0:T(8,128)} %bitcast.170, f32[64,128]{1,0:T(8,128)} %bitcast.172, s32[64,128]{1,0:T(8,128)} %bitcast.165, s32[64,128]{1,0:T(8,128)} %bitcast.154, f32[5,256,256]{2,1,0:T(8,128)} %phase_h.1, ...), custom_call_target="tpu_custom_call" | custom-call | tf_op jit(solution)/shard_map/pallas_call | solution.py:575
  52.6 0.0 copy-done.1
  52.6 0.0 copy-done
  52.6 0.0 copy-done.2
  52.6 0.0 copy-done.5
  52.6 0.0 copy-done.4
  52.6 0.0 copy-done.3
  52.6 0.9 %conditional.1 = (f32[256,512]{1,0:T(8,128)}) conditional(s32[]{:T(128)} %bitcast.23, f32[1024,128]{1,0:T(8,128)S(1)} %get-tuple-element.180, (f32[5,256,256]{2,1,0:T(8,128)S(1)}, s32[8192,1]{0,1:T(1,128)S(1)}, f32[8192]{0:T(1024)S(1)}, f32[8192]{0:T(1024)S(1)}, f32[2,8192]{1,0:T(2,128)S(1)}, /*index=5*/s32[8192]{0:T(1024)S(1)}) %tuple.110), branch_computations={%region_0.0_spmd, %region_1.18_spmd} | conditional | flops 7263794176 | bytes 88359592 | solution.py:641
  52.6 0.9 %reshape.412 = f32[256,512]{1,0:T(8,128)} reshape(f32[1024,128]{1,0:T(8,128)S(1)} %param) | data formatting | bytes 1048576 | tf_op jit(solution)/shard_map/cond/branch_0_fun/reshape | solution.py:642
Async XLA Ops:
  0.0 52.6 %copy-start.1 = (f32[5,256,256]{2,1,0:T(8,128)S(1)}, f32[5,256,256]{2,1,0:T(8,128)}, u32[]{:S(2)}) copy-start(f32[5,256,256]{2,1,0:T(8,128)} %phase_h.1) | copy-start | bytes 3932164
  0.0 52.6 %copy-start = (s32[8192]{0:T(1024)S(1)}, s32[8192]{0:T(1024)}, u32[]{:S(2)}) copy-start(s32[8192]{0:T(1024)} %param.17) | copy-start | bytes 98308
  0.0 52.6 %copy-start.2 = (s32[8192,1]{0,1:T(1,128)S(1)}, s32[8192,1]{0,1:T(1,128)}, u32[]{:S(2)}) copy-start(s32[8192,1]{0,1:T(1,128)} %param.16) | copy-start | bytes 98308
  0.0 52.6 %copy-start.5 = (f32[8192]{0:T(1024)S(1)}, f32[8192]{0:T(1024)}, u32[]{:S(2)}) copy-start(f32[8192]{0:T(1024)} %param.15) | copy-start | bytes 98308
  0.0 52.6 %copy-start.4 = (f32[8192]{0:T(1024)S(1)}, f32[8192]{0:T(1024)}, u32[]{:S(2)}) copy-start(f32[8192]{0:T(1024)} %param.14) | copy-start | bytes 98308
  0.0 52.6 %copy-start.3 = (f32[2,8192]{1,0:T(2,128)S(1)}, f32[2,8192]{1,0:T(2,128)}, u32[]{:S(2)}) copy-start(f32[2,8192]{1,0:T(2,128)} %pos_h.1) | copy-start | bytes 196612

commit v5 on v4

--- a/solution.py
+++ b/solution.py
@@ -348,8 +348,9 @@
     packed_s[...] = jnp.zeros_like(packed_s)
 
     row_128 = lax.broadcasted_iota(jnp.int32, (128, LANES), 0)
-    row_64 = lax.broadcasted_iota(jnp.int32, (64, LANES), 0)
-    row_256f = lax.broadcasted_iota(jnp.int32, (256, LANES), 0).astype(F32)
+    row_64 = lax.broadcasted_iota(jnp.int32, (64, LANES), 0).astype(F32).astype(BF)
+    row_256 = lax.broadcasted_iota(jnp.int32, (256, LANES), 0).astype(F32).astype(BF)
+    one, zero = jnp.asarray(1.0, BF), jnp.asarray(0.0, BF)
     before = lax.broadcasted_iota(jnp.int32, (LANES, 256), 0)
     column = lax.broadcasted_iota(jnp.int32, (LANES, 256), 1)
     counter = jnp.where((before < column) | (column >= LANES), 1.0, 0.0).astype(BF)
@@ -367,8 +368,8 @@
             counts = counts + seen[:, LANES:]
             high_pair = lax.shift_right_logical(pair, 6).astype(F32) * RANKS
             place = jnp.where(rank < RANKS, high_pair + rank, -1.0)
-            right[:, lanes] = jnp.where(row_256f == place, 1.0, 0.0).astype(BF)
-            low_pair = row_64 == lax.bitwise_and(pair, 63)
+            right[:, lanes] = jnp.where(row_256 == place.astype(BF), one, zero)
+            low_pair = row_64 == lax.bitwise_and(pair, 63).astype(F32).astype(BF)
             start = pl.multiple_of(c * LANES, LANES)
             values = (
                 split(pos[0:1, pl.ds(start, LANES)], 3)
@@ -378,7 +379,7 @@
                 + [box_s[pl.ds(c, 1), :]]
             )
             for p, value in enumerate(values):
-                left[p * 64 : (p + 1) * 64, lanes] = jnp.where(low_pair, value, 0.0).astype(BF)
+                left[p * 64 : (p + 1) * 64, lanes] = jnp.where(low_pair, value.astype(BF), zero)
         return counts
 
     def gather(left, right):
@@ -486,15 +487,16 @@
                     high = term.astype(BF)
                     terms[rows_i, lanes] = high
                     terms[rows_i, after] = (term - high.astype(F32)).astype(BF)
-            named = jnp.where(row_256f == field[4][s : s + 1, :], 1.0, 0.0).astype(BF)
-            hot[:, lanes] = named
-            hot[:, after] = named
+            hot[:, lanes] = jnp.where(row_256 == field[4][s : s + 1, :].astype(BF), one, zero)
         return jnp.maximum(largest, field[0])
 
     def one_group(group, largest):
         wait_for(recv_rec, GROUP * FIELDS, rec_recv.at[group])
         largest = build(group, terms_s, hot_s, largest)
-        leaf_s[...] += dot_nt(terms_s[...], hot_s[...])
+        width = GROUP * LANES
+        leaf_s[...] += dot_nt(terms_s[:, :width], hot_s[...]) + dot_nt(
+            terms_s[:, width:], hot_s[...]
+        )
         return largest
 
     largest = lax.fori_loop(0, GROUPS, one_group, jnp.zeros((GROUP, LANES), F32))
@@ -610,7 +612,7 @@
             pltpu.VMEM((Q * GROUP, LANES), F32),
             pltpu.VMEM((Q * GROUP, LANES), F32),
             pltpu.VMEM((512, 2 * GROUP * LANES), BF),
-            pltpu.VMEM((256, 2 * GROUP * LANES), BF),
+            pltpu.VMEM((256, GROUP * LANES), BF),
             pltpu.VMEM((512, 256), F32),
             pltpu.VMEM((256, 512), F32),
             pltpu.VMEM((256, POINTS), F32),

time: 53.6 us -> 51.7 us (0.965)
  Pallas kernels: 51.8 us -> 49.9 us
    pallas_call x1, Pallas kernels: 51.8 us -> 49.9 us  [fast(): pl.pallas_call(body, out_shape=(jax.ShapeDtypeStruct((1024, LANES), F32),...]
where the time goes in v5:
time: 51.7 us; the launch traced here: 51.6 us
  Pallas kernels  49.9 us (97%)
  local copies, waits for them, and re-layouts  0.9 us (2%)
  between operations  0.78 us (2%)
    pallas_call x1, Pallas kernels, fast(): pl.pallas_call(body, out_shape=(jax.ShapeDtypeStruct((1024, LANES), F32),...  49.9 us

profile of v5, /device:TPU:1, one launch (start us, length us, event | category | flops | bytes accessed | tf_op | source)
XLA Modules:
  0.0 51.6 jit_solution(8272775130969437057)
XLA Ops:
  0.0 0.0 copy-start.1
  0.0 0.0 copy-start
  0.0 0.0 copy-start.2
  0.0 0.0 copy-start.5
  0.0 0.0 copy-start.4
  0.0 0.0 copy-start.3
  0.0 49.9 %shard_map.75 = (f32[1024,128]{1,0:T(8,128)S(1)}, f32[1,1]{1,0:T(1,128)}) custom-call(f32[2,8192]{1,0:T(2,128)} %pos_h.1, f32[64,128]{1,0:T(8,128)} %bitcast.170, f32[64,128]{1,0:T(8,128)} %bitcast.172, s32[64,128]{1,0:T(8,128)} %bitcast.165, s32[64,128]{1,0:T(8,128)} %bitcast.154, f32[5,256,256]{2,1,0:T(8,128)} %phase_h.1, ...), custom_call_target="tpu_custom_call" | custom-call | tf_op jit(solution)/shard_map/pallas_call | solution.py:577
  50.6 0.0 copy-done.1
  50.6 0.0 copy-done
  50.7 0.0 copy-done.2
  50.7 0.0 copy-done.5
  50.7 0.0 copy-done.4
  50.7 0.0 copy-done.3
  50.7 0.9 %conditional.1 = (f32[256,512]{1,0:T(8,128)}) conditional(s32[]{:T(128)} %bitcast.23, f32[1024,128]{1,0:T(8,128)S(1)} %get-tuple-element.180, (f32[5,256,256]{2,1,0:T(8,128)S(1)}, s32[8192,1]{0,1:T(1,128)S(1)}, f32[8192]{0:T(1024)S(1)}, f32[8192]{0:T(1024)S(1)}, f32[2,8192]{1,0:T(2,128)S(1)}, /*index=5*/s32[8192]{0:T(1024)S(1)}) %tuple.110), branch_computations={%region_0.0_spmd, %region_1.18_spmd} | conditional | flops 7263794176 | bytes 88359592 | solution.py:643
  50.7 0.9 %reshape.412 = f32[256,512]{1,0:T(8,128)} reshape(f32[1024,128]{1,0:T(8,128)S(1)} %param) | data formatting | bytes 1048576 | tf_op jit(solution)/shard_map/cond/branch_0_fun/reshape | solution.py:644
Async XLA Ops:
  0.0 50.6 %copy-start.1 = (f32[5,256,256]{2,1,0:T(8,128)S(1)}, f32[5,256,256]{2,1,0:T(8,128)}, u32[]{:S(2)}) copy-start(f32[5,256,256]{2,1,0:T(8,128)} %phase_h.1) | copy-start | bytes 3932164
  0.0 50.6 %copy-start = (s32[8192]{0:T(1024)S(1)}, s32[8192]{0:T(1024)}, u32[]{:S(2)}) copy-start(s32[8192]{0:T(1024)} %param.17) | copy-start | bytes 98308
  0.0 50.7 %copy-start.2 = (s32[8192,1]{0,1:T(1,128)S(1)}, s32[8192,1]{0,1:T(1,128)}, u32[]{:S(2)}) copy-start(s32[8192,1]{0,1:T(1,128)} %param.16) | copy-start | bytes 98308
  0.0 50.7 %copy-start.5 = (f32[8192]{0:T(1024)S(1)}, f32[8192]{0:T(1024)}, u32[]{:S(2)}) copy-start(f32[8192]{0:T(1024)} %param.15) | copy-start | bytes 98308
  0.0 50.7 %copy-start.4 = (f32[8192]{0:T(1024)S(1)}, f32[8192]{0:T(1024)}, u32[]{:S(2)}) copy-start(f32[8192]{0:T(1024)} %param.14) | copy-start | bytes 98308
  0.0 50.7 %copy-start.3 = (f32[2,8192]{1,0:T(2,128)S(1)}, f32[2,8192]{1,0:T(2,128)}, u32[]{:S(2)}) copy-start(f32[2,8192]{1,0:T(2,128)} %pos_h.1) | copy-start | bytes 196612

commit v6 on v5

--- a/solution.py
+++ b/solution.py
@@ -31,6 +31,7 @@
 BATCHES = (slice(0, 5),)
 ROW_BITS = ((0, 6), (1, 5), (3, 4), (4, 3), (6, 2), (2, 1), (5, 0))
 STEP_BITS = ((6, 6), (5, 2), (4, 0), (3, 5), (2, 1), (1, 4), (0, 3))
+MIXED_BITS = ((6, 3), (5, 4), (4, 1), (3, 5), (2, 0), (1, 2), (0, 6))
 BF = jnp.bfloat16
 F32 = jnp.float32
 
@@ -257,8 +258,12 @@
     return sum(((number >> source) & 1) << target for source, target in table)
 
 
-GROUP_BITS = tuple((step - 3, bit) for step, bit in STEP_BITS if step >= 3)
-GROUP_ROW_BITS = tuple((step, dict(ROW_BITS)[bit]) for step, bit in GROUP_BITS)
+def group_bits(table):
+    return tuple((step - 3, bit) for step, bit in table if step >= 3)
+
+
+def group_row_bits(table):
+    return tuple((step, dict(ROW_BITS)[bit]) for step, bit in group_bits(table))
 
 
 def dot_nt(left, right):
@@ -284,12 +289,16 @@
     def device(t):
         return {"wide": lax.shift_right_logical(t, 3), "narrow": lax.bitwise_and(t, 7)}
 
-    def for_partners(act):
+    def for_partners(act, table=STEP_BITS):
         def visit(group, first):
-            base = me if first else lax.bitwise_xor(me, move_bits(group, GROUP_BITS))
-            base_row = my_row if first else lax.bitwise_xor(my_row, move_bits(group, GROUP_ROW_BITS))
+            base = me if first else lax.bitwise_xor(me, move_bits(group, group_bits(table)))
+            base_row = (
+                my_row
+                if first
+                else lax.bitwise_xor(my_row, move_bits(group, group_row_bits(table)))
+            )
             for j in range(1 if first else 0, GROUP):
-                offset = move_bits_of(j, STEP_BITS)
+                offset = move_bits_of(j, table)
                 act(
                     group,
                     j,
@@ -443,7 +452,7 @@
                 device_id_type=MESH,
             ).start()
 
-        for_partners(send)
+        for_partners(send, MIXED_BITS)
 
     loads[0].wait()
     for level in range(LEVELS):
@@ -563,7 +572,7 @@
             device_id_type=MESH,
         ).start()
 
-    for_partners(send_results)
+    for_partners(send_results, MIXED_BITS)
     own_out.wait()
     wait_for(out, (DEVICES - 1) * 8, out_recv)
     wait_for(send_rec, (DEVICES - 1) * FIELDS, rec_send)

time: 51.7 us -> 49.9 us (0.965)
  Pallas kernels: 49.9 us -> 48.1 us
    pallas_call x1, Pallas kernels: 49.9 us -> 48.1 us  [fast(): pl.pallas_call(body, out_shape=(jax.ShapeDtypeStruct((1024, LANES), F32),...]
where the time goes in v6:
time: 49.9 us; the launch traced here: 49.7 us
  Pallas kernels  48.1 us (96%)
  local copies, waits for them, and re-layouts  0.9 us (2%)
  between operations  0.78 us (2%)
    pallas_call x1, Pallas kernels, fast(): pl.pallas_call(body, out_shape=(jax.ShapeDtypeStruct((1024, LANES), F32),...  48.1 us

profile of v6, /device:TPU:1, one launch (start us, length us, event | category | flops | bytes accessed | tf_op | source)
XLA Modules:
  0.0 49.7 jit_solution(1899607981650316289)
XLA Ops:
  0.0 0.0 copy-start.1
  0.0 0.0 copy-start
  0.0 0.0 copy-start.2
  0.0 0.0 copy-start.5
  0.0 0.0 copy-start.4
  0.0 0.0 copy-start.3
  0.0 48.1 %shard_map.75 = (f32[1024,128]{1,0:T(8,128)S(1)}, f32[1,1]{1,0:T(1,128)}) custom-call(f32[2,8192]{1,0:T(2,128)} %pos_h.1, f32[64,128]{1,0:T(8,128)} %bitcast.170, f32[64,128]{1,0:T(8,128)} %bitcast.172, s32[64,128]{1,0:T(8,128)} %bitcast.165, s32[64,128]{1,0:T(8,128)} %bitcast.154, f32[5,256,256]{2,1,0:T(8,128)} %phase_h.1, ...), custom_call_target="tpu_custom_call" | custom-call | tf_op jit(solution)/shard_map/pallas_call | solution.py:586
  48.8 0.0 copy-done.1
  48.8 0.0 copy-done
  48.8 0.0 copy-done.2
  48.8 0.0 copy-done.5
  48.8 0.0 copy-done.4
  48.9 0.0 copy-done.3
  48.9 0.9 %conditional.1 = (f32[256,512]{1,0:T(8,128)}) conditional(s32[]{:T(128)} %bitcast.23, f32[1024,128]{1,0:T(8,128)S(1)} %get-tuple-element.180, (f32[5,256,256]{2,1,0:T(8,128)S(1)}, s32[8192,1]{0,1:T(1,128)S(1)}, f32[8192]{0:T(1024)S(1)}, f32[8192]{0:T(1024)S(1)}, f32[2,8192]{1,0:T(2,128)S(1)}, /*index=5*/s32[8192]{0:T(1024)S(1)}) %tuple.110), branch_computations={%region_0.0_spmd, %region_1.18_spmd} | conditional | flops 7263794176 | bytes 88359592 | solution.py:652
  48.9 0.9 %reshape.412 = f32[256,512]{1,0:T(8,128)} reshape(f32[1024,128]{1,0:T(8,128)S(1)} %param) | data formatting | bytes 1048576 | tf_op jit(solution)/shard_map/cond/branch_0_fun/reshape | solution.py:653
Async XLA Ops:
  0.0 48.8 %copy-start.1 = (f32[5,256,256]{2,1,0:T(8,128)S(1)}, f32[5,256,256]{2,1,0:T(8,128)}, u32[]{:S(2)}) copy-start(f32[5,256,256]{2,1,0:T(8,128)} %phase_h.1) | copy-start | bytes 3932164
  0.0 48.8 %copy-start = (s32[8192]{0:T(1024)S(1)}, s32[8192]{0:T(1024)}, u32[]{:S(2)}) copy-start(s32[8192]{0:T(1024)} %param.17) | copy-start | bytes 98308
  0.0 48.8 %copy-start.2 = (s32[8192,1]{0,1:T(1,128)S(1)}, s32[8192,1]{0,1:T(1,128)}, u32[]{:S(2)}) copy-start(s32[8192,1]{0,1:T(1,128)} %param.16) | copy-start | bytes 98308
  0.0 48.8 %copy-start.5 = (f32[8192]{0:T(1024)S(1)}, f32[8192]{0:T(1024)}, u32[]{:S(2)}) copy-start(f32[8192]{0:T(1024)} %param.15) | copy-start | bytes 98308
  0.0 48.8 %copy-start.4 = (f32[8192]{0:T(1024)S(1)}, f32[8192]{0:T(1024)}, u32[]{:S(2)}) copy-start(f32[8192]{0:T(1024)} %param.14) | copy-start | bytes 98308
  0.0 48.8 %copy-start.3 = (f32[2,8192]{1,0:T(2,128)S(1)}, f32[2,8192]{1,0:T(2,128)}, u32[]{:S(2)}) copy-start(f32[2,8192]{1,0:T(2,128)} %pos_h.1) | copy-start | bytes 196612
